TPU v7x, 32 devices: a whole 2x2x4 slice. The times are simulated.
32 devices in a mesh: subset: 4 (over y, x), tile: 8 (over z, core).
Axes of the slice: x: 2, y: 2, z: 4, core: 2. Of those that a mesh axis runs over, the one named last changes fastest.
Arguments:
- start_volume: bfloat16 [4, 64, 32768], P(None, None, 'tile'), may hold values from 0 to 2
- measured: bfloat16 [4, 4, 64, 2048], P('subset'), may hold values from 3264 to 13056
- system_values: bfloat16 [4, 2048, 32768], P('subset', None, 'tile'), may hold values from 0.05 to 2088.96, as said below
- block_pattern: int32 [4, 16, 256], P('subset', None, 'tile'), may hold values from 0 to 1, as said below
- subset_order: int32 [64, 4], replicated, may hold values from 0 to 3, each once within a row
Outputs:
- volume_out: bfloat16 [4, 64, 32768], P(None, None, 'tile')
Inputs may be any that keep to these rules, and one draw needn't show every extreme that they name: `block_pattern`: each entry is 0 or 1; every block row and every block column of each subset's matrix within every 4096-voxel tile holds at least one 1. `system_values`: positive entries. `subset_order`: each row is a permutation of the 4 subsets.
All inputs are finite; a program needn't handle non-finite values.
Results may differ from a plain program's by a relative error of at most 0.0034.
Values may be sent and summed in bfloat16 or wider, within the bound.
No kernel may reach another device: no remote copies, remote signals or barrier semaphores. Data moves between devices by JAX's collectives and lax.ppermute only.
A program may use at most 128 MiB of HBM per device.

v0:
```python
import jax
import jax.numpy as jnp
from jax import lax
from jax.sharding import PartitionSpec as P

BLOCK_SIDE = 128
SWEEP_PASSES = 4


def passed_along(block, axis, distance):
    devices = range(lax.axis_size(axis))
    route = [((i - distance) % len(devices), i) for i in devices]
    return lax.ppermute(block, axis, route)


def body(start_volume, measured, system_values, block_pattern, subset_order):
    owner_idx = lax.axis_index("subset")
    holder_count = lax.axis_size("subset")
    tile_count = lax.axis_size("tile")
    pattern = block_pattern[0].astype(jnp.bfloat16)
    matrix = system_values[0] * jnp.repeat(jnp.repeat(pattern, BLOCK_SIDE, 0), BLOCK_SIDE, 1)
    column_sum = jnp.sum(matrix, axis=0, dtype=jnp.float32)
    row_part = jnp.sum(matrix, axis=1, dtype=jnp.float32)[None, :]
    slice_measurement = measured[0]
    ray_width = matrix.shape[0]
    row_share_list = ray_width // tile_count
    row_displacement = lax.axis_index("tile") * row_share_list

    def subset_selector(slice_portion):
        source = (owner_idx - slice_portion) % holder_count
        return (subset_order == source).astype(jnp.bfloat16)

    volume = jnp.einsum(
        "sf,fsv->sv", subset_selector(0), start_volume, preferred_element_type=jnp.float32
    )
    ray_total = lax.psum_scatter(row_part, "tile", scatter_dimension=1, tiled=True)
    for slice_portion in range(SWEEP_PASSES):
        selected_subset = subset_selector(slice_portion)
        destination_rows = jnp.einsum(
            "ej,jev->ev", selected_subset, slice_measurement, preferred_element_type=jnp.float32
        )
        narrow = volume.astype(jnp.bfloat16)
        partial_value = lax.dot_general(
            narrow, matrix, (((1,), (1,)), ((), ())), preferred_element_type=jnp.float32
        )
        projected = lax.psum_scatter(partial_value, "tile", scatter_dimension=1, tiled=True)
        target_share = lax.dynamic_slice_in_dim(
            destination_rows, row_displacement, row_share_list, 1
        )
        residue = ((target_share - projected) / ray_total).astype(jnp.bfloat16)
        spread_back = jnp.dot(
            lax.all_gather(residue, "tile", axis=1, tiled=True),
            matrix,
            preferred_element_type=jnp.float32,
        )
        volume = volume + spread_back / column_sum[None, :]
        if slice_portion + 1 < SWEEP_PASSES:
            volume = passed_along(volume, "subset", 1)
    final_pick = subset_selector(SWEEP_PASSES - 1).astype(jnp.float32)
    rounded = lax.optimization_barrier(volume.astype(jnp.bfloat16)).astype(jnp.float32)
    contribution = jnp.transpose(final_pick)[:, :, None] * rounded[None, :, :]
    gathered = lax.psum(contribution.astype(jnp.bfloat16), "subset")
    return gathered


def solution(mesh):
    placed = (
        P(None, None, "tile"),
        P("subset", None, None, None),
        P("subset", None, "tile"),
        P("subset", None, "tile"),
        P(),
    )
    return jax.shard_map(
        body, mesh=mesh, in_specs=placed, out_specs=P(None, None, "tile"), check_vma=False
    )
```

profile of v0, /device:TPU:0, one launch (start us, length us, event | category | flops | bytes accessed | tf_op | source)
XLA Modules:
  0.0 491.2 jit_solution(13172563963217522324)
XLA Ops:
  7.5 25.4 %broadcast_in_dim.7 = bf16[2048,32,128]{2,1,0:T(8,128)(2,1)S(1)} broadcast(bf16[2048,32]{1,0:T(8,128)(2,1)S(1)} %bitcast.59), dimensions={0,1} | broadcast | bytes 16908288 | tf_op jit(solution)/shard_map/broadcast_in_dim | solution.py:21
  32.9 13.7 %convert_reduce_fusion = (f32[4096]{0:T(1024)S(1)}, f32[2048]{0:T(1024)S(1)}, bf16[2048,4096]{1,0:T(8,128)(2,1)}) fusion(bf16[256,8,32,128]{3,2,1,0:T(8,128)(2,1)S(1)} %bitcast.57, bf16[1,2048,4096]{2,1,0:T(8,128)(2,1)} %param.7), kind=kLoop, calls=%fused_computation | loop fusion | flops 33548288 | bytes 50356224 | tf_op jit(solution)/shard_map/reduce_sum | solution.py:22
  46.6 1.3 copy.17
  48.2 1.9 fusion.5
  50.2 11.9 %fusion.7 = f32[64,2048]{1,0:T(8,128)} fusion(bf16[2048,4096]{1,0:T(8,128)(2,1)} %get-tuple-element.9, f32[64,1,4096]{2,1,0:T(1,128)S(1)} %fusion.5), kind=kOutput, calls=%fused_computation.16 | convolution fusion | flops 1073741824 | bytes 18350080 | tf_op jit(solution)/shard_map/dot_general | solution.py:43
  62.1 2.1 fusion.20
  64.4 18.7 %reduce-scatter.16.cloned.1.call-done = f32[256,1]{1,0:T(8,128)} async-done(((f32[2048,1]{1,0:T(8,128)}), f32[256,1]{1,0:T(8,128)}) %reduce-scatter.16.cloned.1.call-update) | async-done | bytes 1040
  84.1 30.5 %reduce-scatter.8.cloned.1.call-done = f32[64,256]{1,0:T(8,128)} async-done(((f32[64,2048]{1,0:T(8,128)}), f32[64,256]{1,0:T(8,128)}) %reduce-scatter.8.cloned.1.call-update) | async-done | bytes 65552 | tf_op jit(solution)/shard_map/reduce_scatter | solution.py:46
  115.4 14.4 %all_gather.12 = bf16[64,2048]{1,0:T(8,128)(2,1)S(1)} all-gather(bf16[64,256]{1,0:T(8,128)(2,1)S(1)} %divide_convert_fusion.3), channel_id=1, replica_groups=mesh['subset'=4,'tile'=8] {'tile'}, dimensions={1}, use_global_device_ids=true | all-gather | bytes 294912 | tf_op jit(solution)/shard_map/all_gather | solution.py:52
  129.8 9.4 %fusion.3 = f32[64,4096]{1,0:T(8,128)S(1)} fusion(bf16[64,2048]{1,0:T(8,128)(2,1)S(1)} %all_gather.12, bf16[2048,4096]{1,0:T(8,128)(2,1)} %get-tuple-element.9, f32[64,1,4096]{2,1,0:T(1,128)S(1)} %fusion.5, f32[4096]{0:T(1024)S(1)} %get-tuple-element.5), kind=kOutput, calls=%fused_computation.10 | convolution fusion | flops 1074266112 | bytes 19152896 | tf_op jit(solution)/shard_map/dot_general | solution.py:51
  139.2 1.6 collective-permute-start
  140.8 24.8 %collective-permute-done = f32[64,4096]{1,0:T(8,128)S(1)} collective-permute-done((f32[64,4096]{1,0:T(8,128)S(1)}, f32[64,4096]{1,0:T(8,128)S(1)}, u32[]{:S(2)}, u32[]{:S(2)}) %collective-permute-start) | collective-permute-done | bytes 1048608 | tf_op jit(solution)/shard_map/ppermute | solution.py:13
  165.6 11.8 %fusion.12 = f32[64,2048]{1,0:T(8,128)} fusion(bf16[2048,4096]{1,0:T(8,128)(2,1)} %get-tuple-element.9, f32[64,4096]{1,0:T(8,128)S(1)} %collective-permute-done), kind=kOutput, calls=%fused_computation.25 | convolution fusion | flops 1074003968 | bytes 18350080 | tf_op jit(solution)/shard_map/dot_general | solution.py:43
  178.6 27.1 %reduce-scatter.10.cloned.1.call-done = f32[64,256]{1,0:T(8,128)} async-done(((f32[64,2048]{1,0:T(8,128)}), f32[64,256]{1,0:T(8,128)}) %reduce-scatter.10.cloned.1.call-update) | async-done | bytes 65552 | tf_op jit(solution)/shard_map/reduce_scatter | solution.py:46
  206.6 14.2 %all_gather.13 = bf16[64,2048]{1,0:T(8,128)(2,1)S(1)} all-gather(bf16[64,256]{1,0:T(8,128)(2,1)S(1)} %divide_convert_fusion.2), channel_id=1, replica_groups=mesh['subset'=4,'tile'=8] {'tile'}, dimensions={1}, use_global_device_ids=true | all-gather | bytes 294912 | tf_op jit(solution)/shard_map/all_gather | solution.py:52
  220.8 8.8 %fusion.2 = f32[64,4096]{1,0:T(8,128)S(1)} fusion(f32[64,4096]{1,0:T(8,128)S(1)} %collective-permute-done, bf16[64,2048]{1,0:T(8,128)(2,1)S(1)} %all_gather.13, bf16[2048,4096]{1,0:T(8,128)(2,1)} %get-tuple-element.9, f32[4096]{0:T(1024)S(1)} %get-tuple-element.5), kind=kOutput, calls=%fused_computation.8 | convolution fusion | flops 1074266112 | bytes 19152896 | tf_op jit(solution)/shard_map/dot_general | solution.py:51
  229.6 1.8 collective-permute-start.1
  231.4 24.8 %collective-permute-done.1 = f32[64,4096]{1,0:T(8,128)S(1)} collective-permute-done((f32[64,4096]{1,0:T(8,128)S(1)}, f32[64,4096]{1,0:T(8,128)S(1)}, u32[]{:S(2)}, u32[]{:S(2)}) %collective-permute-start.1) | collective-permute-done | bytes 1048608 | tf_op jit(solution)/shard_map/ppermute | solution.py:13
  256.2 11.8 %fusion.10 = f32[64,2048]{1,0:T(8,128)} fusion(bf16[2048,4096]{1,0:T(8,128)(2,1)} %get-tuple-element.9, f32[64,4096]{1,0:T(8,128)S(1)} %collective-permute-done.1), kind=kOutput, calls=%fused_computation.23 | convolution fusion | flops 1074003968 | bytes 18350080 | tf_op jit(solution)/shard_map/dot_general | solution.py:43
  269.3 27.2 %reduce-scatter.12.cloned.1.call-done = f32[64,256]{1,0:T(8,128)} async-done(((f32[64,2048]{1,0:T(8,128)}), f32[64,256]{1,0:T(8,128)}) %reduce-scatter.12.cloned.1.call-update) | async-done | bytes 65552 | tf_op jit(solution)/shard_map/reduce_scatter | solution.py:46
  297.3 14.2 %all_gather.14 = bf16[64,2048]{1,0:T(8,128)(2,1)S(1)} all-gather(bf16[64,256]{1,0:T(8,128)(2,1)S(1)} %divide_convert_fusion.1), channel_id=1, replica_groups=mesh['subset'=4,'tile'=8] {'tile'}, dimensions={1}, use_global_device_ids=true | all-gather | bytes 294912 | tf_op jit(solution)/shard_map/all_gather | solution.py:52
  311.5 8.8 %fusion.1 = f32[64,4096]{1,0:T(8,128)S(1)} fusion(f32[64,4096]{1,0:T(8,128)S(1)} %collective-permute-done.1, bf16[64,2048]{1,0:T(8,128)(2,1)S(1)} %all_gather.14, bf16[2048,4096]{1,0:T(8,128)(2,1)} %get-tuple-element.9, f32[4096]{0:T(1024)S(1)} %get-tuple-element.5), kind=kOutput, calls=%fused_computation.6 | convolution fusion | flops 1074266112 | bytes 19152896 | tf_op jit(solution)/shard_map/dot_general | solution.py:51
  320.3 1.7 collective-permute-start.2
  322.0 24.7 %collective-permute-done.2 = f32[64,4096]{1,0:T(8,128)S(1)} collective-permute-done((f32[64,4096]{1,0:T(8,128)S(1)}, f32[64,4096]{1,0:T(8,128)S(1)}, u32[]{:S(2)}, u32[]{:S(2)}) %collective-permute-start.2) | collective-permute-done | bytes 1048608 | tf_op jit(solution)/shard_map/ppermute | solution.py:13
  346.7 11.8 %fusion.8 = f32[64,2048]{1,0:T(8,128)} fusion(bf16[2048,4096]{1,0:T(8,128)(2,1)} %get-tuple-element.9, f32[64,4096]{1,0:T(8,128)S(1)} %collective-permute-done.2), kind=kOutput, calls=%fused_computation.21 | convolution fusion | flops 1074003968 | bytes 18350080 | tf_op jit(solution)/shard_map/dot_general | solution.py:43
  358.9 2.1 fusion.14
  361.2 25.7 %reduce-scatter.14.cloned.1.call-done = f32[64,256]{1,0:T(8,128)} async-done(((f32[64,2048]{1,0:T(8,128)}), f32[64,256]{1,0:T(8,128)}) %reduce-scatter.14.cloned.1.call-update) | async-done | bytes 65552 | tf_op jit(solution)/shard_map/reduce_scatter | solution.py:46
  387.7 14.3 %all_gather.15 = bf16[64,2048]{1,0:T(8,128)(2,1)S(1)} all-gather(bf16[64,256]{1,0:T(8,128)(2,1)S(1)} %divide_convert_fusion), channel_id=1, replica_groups=mesh['subset'=4,'tile'=8] {'tile'}, dimensions={1}, use_global_device_ids=true | all-gather | bytes 294912 | tf_op jit(solution)/shard_map/all_gather | solution.py:52
  402.1 8.8 %fusion.4 = bf16[64,4096]{1,0:T(8,128)(2,1)S(1)} fusion(f32[64,4096]{1,0:T(8,128)S(1)} %collective-permute-done.2, bf16[64,2048]{1,0:T(8,128)(2,1)S(1)} %all_gather.15, bf16[2048,4096]{1,0:T(8,128)(2,1)} %get-tuple-element.9, f32[4096]{0:T(1024)S(1)} %get-tuple-element.5), kind=kOutput, calls=%fused_computation.11 | convolution fusion | flops 1074528256 | bytes 18628608 | tf_op jit(solution)/shard_map/dot_general | solution.py:51
  411.0 1.7 multiply_convert_fusion
  412.7 68.0 %all-reduce.2.cloned.1.call-done = bf16[4,64,4096]{2,1,0:T(8,128)(2,1)} async-done(((bf16[4,64,4096]{2,1,0:T(8,128)(2,1)}), bf16[4,64,4096]{2,1,0:T(8,128)(2,1)}) %all-reduce.2.cloned.1.call-update) | async-done | bytes 2097168 | tf_op jit(solution)/shard_map/psum | solution.py:62
  480.8 3.1 copy.44
  (39 shorter events, 9.0 us)
Async XLA Ops:
  6.5 41.7 %copy-start = (bf16[4,64,4096]{2,1,0:T(8,128)(2,1)S(1)}, bf16[4,64,4096]{2,1,0:T(8,128)(2,1)}, u32[]{:S(2)}) copy-start(bf16[4,64,4096]{2,1,0:T(8,128)(2,1)} %param.5) | copy-start | bytes 6291460
  6.5 76.6 %reduce-scatter.16.cloned.1.call-start = ((), (), s32[]{:S(2)}) async-start(), calls=%async_computation.10 | async-start | bytes 1179648
  32.9 15.2 %copy-start.2 = (s32[64,4]{0,1:T(4,128)S(1)}, s32[64,4]{0,1:T(4,128)}, u32[]{:S(2)}) copy-start(s32[64,4]{0,1:T(4,128)} %param.9) | copy-start | bytes 3076
  47.9 66.6 %reduce-scatter.8.cloned.1.call-start = ((), (), s32[]{:S(2)}) async-start(), calls=%async_computation.5 | async-start | bytes 589824 | tf_op jit(solution)/shard_map/reduce_scatter | solution.py:46
  62.0 143.7 %reduce-scatter.10.cloned.1.call-start = ((), (), s32[]{:S(2)}) async-start(), calls=%async_computation.6 | async-start | bytes 589824 | tf_op jit(solution)/shard_map/reduce_scatter | solution.py:46
  139.2 38.3 %copy-start.3 = (bf16[1,4,64,2048]{3,2,1,0:T(8,128)(2,1)S(1)}, bf16[1,4,64,2048]{3,2,1,0:T(8,128)(2,1)}, u32[]{:S(2)}) copy-start(bf16[1,4,64,2048]{3,2,1,0:T(8,128)(2,1)} %param.6) | copy-start | bytes 3145732
  139.2 26.4 %collective-permute-start = (f32[64,4096]{1,0:T(8,128)S(1)}, f32[64,4096]{1,0:T(8,128)S(1)}, u32[]{:S(2)}, u32[]{:S(2)}) collective-permute-start(f32[64,4096]{1,0:T(8,128)S(1)} %fusion.3), channel_id=1, source_target_pairs={{24,0},{0,8},{8,16},{16,24},{25,1},{1,9},{9,17},{17,25},{26,2},{2,... | collective-permute-start | bytes 3145736 | tf_op jit(solution)/shard_map/ppermute | solution.py:13
  177.3 119.1 %reduce-scatter.12.cloned.1.call-start = ((), (), s32[]{:S(2)}) async-start(), calls=%async_computation.7 | async-start | bytes 589824 | tf_op jit(solution)/shard_map/reduce_scatter | solution.py:46
  229.6 26.6 %collective-permute-start.1 = (f32[64,4096]{1,0:T(8,128)S(1)}, f32[64,4096]{1,0:T(8,128)S(1)}, u32[]{:S(2)}, u32[]{:S(2)}) collective-permute-start(f32[64,4096]{1,0:T(8,128)S(1)} %fusion.2), channel_id=1, source_target_pairs={{24,0},{0,8},{8,16},{16,24},{25,1},{1,9},{9,17},{17,25},{26,2},{2,... | collective-permute-start | bytes 3145736 | tf_op jit(solution)/shard_map/ppermute | solution.py:13
  268.0 118.9 %reduce-scatter.14.cloned.1.call-start = ((), (), s32[]{:S(2)}) async-start(), calls=%async_computation.8 | async-start | bytes 589824 | tf_op jit(solution)/shard_map/reduce_scatter | solution.py:46
  320.3 26.4 %collective-permute-start.2 = (f32[64,4096]{1,0:T(8,128)S(1)}, f32[64,4096]{1,0:T(8,128)S(1)}, u32[]{:S(2)}, u32[]{:S(2)}) collective-permute-start(f32[64,4096]{1,0:T(8,128)S(1)} %fusion.1), channel_id=1, source_target_pairs={{24,0},{0,8},{8,16},{16,24},{25,1},{1,9},{9,17},{17,25},{26,2},{2,... | collective-permute-start | bytes 3145736 | tf_op jit(solution)/shard_map/ppermute | solution.py:13
  358.4 122.3 %all-reduce.2.cloned.1.call-start = ((), (), s32[]{:S(2)}) async-start(), calls=%async_computation.9 | async-start | bytes 4194304 | tf_op jit(solution)/shard_map/psum | solution.py:62
  387.7 96.1 %copy-start.1 = (bf16[4,64,4096]{2,1,0:T(8,128)(2,1)S(1)}, bf16[4,64,4096]{2,1,0:T(8,128)(2,1)}, u32[]{:S(2)}) copy-start(bf16[4,64,4096]{2,1,0:T(8,128)(2,1)} %param.5) | copy-start | bytes 6291460
Sparse Core Ops, SparseCore 0:
  48.1 35.0 reduce-scatter.15
  85.4 29.1 reduce-scatter.7
  177.5 28.2 reduce-scatter.9
  268.1 28.2 reduce-scatter.11
  358.6 28.2 reduce-scatter.13
  412.8 67.8 all-reduce.1
where the time goes:
time: 499 us; the launch traced here: 491 us
  waiting for transfers between devices  272 us (55%)
  matrix products  91 us (18%)
  blocking collectives  57.1 us (11%)
  local copies, waits for them, and re-layouts  32.2 us (6%)
  other arithmetic  19.7 us (4%)
  between operations  14.2 us (3%)
  starting transfers between devices  5.51 us (1%)
    reduce_scatter x4, waiting for transfers between devices, body(): lax.psum_scatter(partial_value, 'tile', scatter_dimension=1, tiled=True)  110 us
    ppermute x3, waiting for transfers between devices, passed_along(): return lax.ppermute(block, axis, route)  74.2 us
    psum x1, waiting for transfers between devices, body(): gathered = lax.psum(contribution.astype(jnp.bfloat16), 'subset')  68 us
    all_gather x4, blocking collectives, body(): lax.all_gather(residue, 'tile', axis=1, tiled=True)  57.1 us
    dot_general x4, matrix products, body(): lax.dot_general(narrow, matrix, (((1,), (1,)), ((), ())), preferred_eleme...  47.1 us
    dot_general x4, matrix products, body(): jnp.dot(lax.all_gather(residue, 'tile', axis=1, tiled=True), matrix, pref...  35.9 us
    broadcast_in_dim x1, local copies, waits for them, and re-layouts, body(): jnp.repeat(jnp.repeat(pattern, BLOCK_SIDE, 0), BLOCK_SIDE, 1)  25.4 us
    unnamed x7, waiting for transfers between devices  18.8 us
  transfers between devices with their start and end apart: 9, of which 9 were waited for; matrix products, arithmetic and copies ran while one was open for 4% of the time, Pallas kernels for 0%

commit v1 on v0

v1 whole, which is shorter than its diff:
```python
import functools

import jax
import jax.numpy as jnp
from jax import lax
from jax.experimental import pallas as pl
from jax.experimental.pallas import tpu as pltpu
from jax.sharding import PartitionSpec as P

F32, BF16, F16 = jnp.float32, jnp.bfloat16, jnp.float16
RAY_SCALE = 2.0**-14
EXTRA = 16
CHUNKS = 2
LOADS = 8
VM = pl.BlockSpec(memory_space=pltpu.VMEM)
SM = pl.BlockSpec(memory_space=pltpu.SMEM)


def call(kernel, out_shape, args, specs, flops, name, scratch=(), vmem=8 << 20):
    out_specs = jax.tree.map(lambda _: VM, out_shape)
    return pl.pallas_call(
        kernel,
        out_shape=out_shape,
        in_specs=specs,
        out_specs=out_specs,
        scratch_shapes=scratch,
        name=name,
        cost_estimate=pl.CostEstimate(flops=flops, bytes_accessed=flops // 64, transcendentals=0),
        compiler_params=pltpu.CompilerParams(vmem_limit_bytes=vmem),
    )(*args)


def shaped(shape, dtype=F32):
    return jax.ShapeDtypeStruct(shape, dtype)


def dot_nt(a, b):
    return lax.dot_general(a, b, (((1,), (1,)), ((), ())), preferred_element_type=F32)


def dot_nn(a, b):
    return lax.dot_general(a, b, (((1,), (0,)), ((), ())), preferred_element_type=F32)


def load_kernel(matrix_hbm, pattern, volume, matrix, rays, sems):
    ray_blocks, col_blocks = pattern.shape
    ray_count, voxels = matrix.shape
    side = ray_count // ray_blocks
    rows = ray_count // LOADS
    per_load = ray_blocks // LOADS

    def piece(i):
        where = pl.ds(i * rows, rows)
        return pltpu.make_async_copy(matrix_hbm.at[where], matrix.at[where], sems.at[i])

    for i in range(LOADS):
        piece(i).start()

    @pl.loop(0, LOADS)
    def _(i):
        piece(i).wait()
        for r in range(per_load):
            block_row = i * per_load + r
            where = pl.ds(pl.multiple_of(block_row * side, side), side)
            for c in range(col_blocks):
                cols = slice(c * side, (c + 1) * side)
                keep = pattern[block_row, c] != 0
                block = matrix[where, cols]
                matrix[where, cols] = jnp.where(keep, block, jnp.zeros_like(block))
        where = pl.ds(pl.multiple_of(i * rows, rows), rows)
        rays[:, where] = dot_nt(volume[...], matrix[where, :])


def project_first(volume, matrix, rays):
    width = volume.shape[1]
    rays[...] = dot_nt(volume[...], matrix[:, :width])


def project_half(half, volume, so_far, matrix, rays):
    width = volume.shape[1]
    count = rays.shape[1]
    where = pl.ds(pl.multiple_of(half[0] * count, count), count)
    rays[...] = so_far[:, where] + dot_nt(volume[...], matrix[where, matrix.shape[1] - width :])


def spread_first(half, residue, matrix, spread):
    count = residue.shape[1]
    where = pl.ds(pl.multiple_of(half[0] * count, count), count)
    spread[...] = dot_nn(residue[...], matrix[where, :])


def spread_last(chunk, first, half, residue, so_far, volume, column, matrix, out, *column_out):
    count = residue.shape[1]
    slices, width = out.shape
    cols = slice(chunk * width, (chunk + 1) * width)
    where = pl.ds(pl.multiple_of(half[0] * count, count), count)
    total = so_far[:, cols] + dot_nn(residue[...], matrix[where, cols])
    if first:
        inverse = 1.0 / total[slices : slices + 1, :]
        column_out[0][...] = inverse
    else:
        inverse = column[...]
    out[...] = volume[...] + total[:slices] * inverse


def passed(x, axis, distance):
    size = lax.axis_size(axis)
    return lax.ppermute(x, axis, [(i, (i + distance) % size) for i in range(size)])


def swapped(x, axis, bit):
    size = lax.axis_size(axis)
    return lax.ppermute(x, axis, [(i, i ^ bit) for i in range(size)])


def tile_sum(own, received):
    total = own + received.astype(F32)
    bit = 2
    while bit < lax.axis_size("tile"):
        total = total + swapped(total.astype(F16), "tile", bit).astype(F32)
        bit *= 2
    return total


def from_all_owners(chunks):
    owner = lax.axis_index("subset")
    owners = lax.axis_size("subset")
    found = [(owner, chunks)]
    if owners == 4 and len(chunks) == 2:
        near = [swapped(c, "subset", 1) for c in chunks]
        far = [swapped(c, "subset", 2) for c in chunks]
        both = [swapped(far[0], "subset", 1), swapped(near[1], "subset", 2)]
        return found + [(owner ^ 1, near), (owner ^ 2, far), (owner ^ 3, both)]
    for d in range(1, owners):
        found.append(((owner - d) % owners, [passed(c, "subset", d) for c in chunks]))
    return found


def body(start_volume, measured, system_values, block_pattern, subset_order):
    owner = lax.axis_index("subset")
    owners = lax.axis_size("subset")
    core = lax.axis_index("tile") % 2
    own, other = [jnp.reshape(h, (1,)).astype(jnp.int32) for h in (core, 1 - core)]
    fronts, slices, voxels = start_volume.shape
    ray_count = measured.shape[-1]
    half = ray_count // 2
    width = voxels // CHUNKS
    passes = owners

    def mine(j):
        return (subset_order + j) % owners == owner

    def pick(j, parts):
        chosen = mine(j)
        got = parts[0]
        for f in range(1, fronts):
            got = jnp.where(chosen[:, f : f + 1], parts[f], got)
        return got

    start = pick(0, start_volume)
    ones = jnp.ones((EXTRA, voxels), BF16)
    matrix, rays = call(
        load_kernel,
        (pltpu.VMEM((ray_count, voxels), BF16), shaped((slices + EXTRA, ray_count))),
        (system_values[0], block_pattern[0], jnp.concatenate([start, ones])),
        [pl.BlockSpec(memory_space=pltpu.HBM), SM, VM],
        2 * slices * ray_count * voxels,
        "load_and_project",
        scratch=[pltpu.SemaphoreType.DMA((LOADS,))],
    )
    my_rays = lax.dynamic_slice_in_dim(measured[0], core * half, half, 2)
    volume = [start[:, c * width : (c + 1) * width].astype(F32) for c in range(CHUNKS)]
    column = [None] * CHUNKS
    inverse_row = None
    work = 2 * slices * ray_count * voxels
    for j in range(passes):
        if j == 0:
            rest = lax.dynamic_slice_in_dim(rays, (1 - core) * half, half, 1)
            kept = lax.dynamic_slice_in_dim(rays, core * half, half, 1)
        else:
            narrow = [v.astype(BF16) for v in volume]
            so_far = call(
                project_first, shaped((slices, ray_count)), (narrow[0], matrix), [VM, VM],
                work // 2, "project_first",
            )
            rest, kept = [
                call(
                    project_half, shaped((slices, half)), (h, narrow[1], so_far, matrix),
                    [SM, VM, VM, VM], work // 4, "project_half",
                )
                for h in (other, own)
            ]
        received = swapped((rest * RAY_SCALE).astype(F16), "tile", 1)
        total = tile_sum(kept * RAY_SCALE, received)
        if j == 0:
            inverse_row = 1.0 / total[slices : slices + 1]
            total = total[:slices]
        target = pick(j, my_rays).astype(F32) * RAY_SCALE
        residue = ((target - total) * inverse_row).astype(BF16)
        if j == 0:
            residue = jnp.concatenate([residue, jnp.ones((EXTRA, half), BF16)])
        rest_residue = swapped(residue, "tile", 1)
        spread = call(
            spread_first, shaped((residue.shape[0], voxels)), (own, residue, matrix),
            [SM, VM, VM], work // 2, "spread_first",
        )
        for c in range(CHUNKS):
            shapes = [shaped((slices, width))]
            if j == 0:
                shapes.append(shaped((1, width)))
                prior = jnp.zeros((1, width), F32)
            else:
                prior = column[c]
            got = call(
                functools.partial(spread_last, c, j == 0), tuple(shapes),
                (other, rest_residue, spread, volume[c], prior, matrix),
                [SM, VM, VM, VM, VM, VM], work // 4, "spread_last",
            )
            volume[c] = got[0]
            if j == 0:
                column[c] = got[1]
        if j + 1 < passes:
            volume = [passed(v.astype(F16), "subset", 1).astype(F32) for v in volume]

    found = from_all_owners([v.astype(BF16) for v in volume])
    last_owner = jnp.transpose((subset_order + passes - 1) % owners)[:, :, None]
    outs = []
    for c in range(CHUNKS):
        got = jnp.broadcast_to(found[0][1][c][None], (fronts, slices, width))
        for who, chunks in found[1:]:
            got = jnp.where(last_owner == who, chunks[c][None], got)
        outs.append(got)
    return jnp.concatenate(outs, axis=2)


def solution(mesh):
    placed = (
        P(None, None, "tile"),
        P("subset", None, None, None),
        P("subset", None, "tile"),
        P("subset", None, "tile"),
        P(),
    )
    return jax.shard_map(
        body, mesh=mesh, in_specs=placed, out_specs=P(None, None, "tile"), check_vma=False
    )
```

time: 499 us -> 192 us (0.38); the launches traced: 491 us -> 191 us
  waiting for transfers between devices: 272 us -> 88.1 us
  matrix products: 91 us -> 0 us
  blocking collectives: 57.1 us -> 0 us
  Pallas kernels: 0 us -> 42.8 us
  starting transfers between devices: 5.51 us -> 31.2 us
  between operations: 14.2 us -> 0.57 us
  other arithmetic: 19.7 us -> 7.06 us
  local copies, waits for them, and re-layouts: 32.2 us -> 21.5 us
    reduce_scatter x4 -> x0, waiting for transfers between devices: 110 us -> none  [body(): lax.psum_scatter(partial_value, 'tile', scatter_dimension=1, tiled=True)]
    dot_general x13 -> x0, matrix products: 91 us -> none  [the longest x4 47.1 us: body(): lax.dot_general(narrow, matrix, (((1,), (1,)), ((), ())), preferred_eleme...]
    psum x1 -> x0, waiting for transfers between devices: 68 us -> none  [body(): gathered = lax.psum(contribution.astype(jnp.bfloat16), 'subset')]
    all_gather x4 -> x0, blocking collectives: 57.1 us -> none  [body(): lax.all_gather(residue, 'tile', axis=1, tiled=True)]
    pallas_call x0 -> x22, Pallas kernels: none -> 42.8 us  [call(): pl.pallas_call(kernel, out_shape=out_shape, in_specs=specs, out_specs=out...]
    ppermute x3 -> x28, starting transfers between devices: 5.05 us -> 31.2 us  [the longest x22 22.1 us: swapped(): return lax.ppermute(x, axis, [(i, i ^ bit) for i in range(size)])]
    broadcast_in_dim x2 -> x4, local copies, waits for them, and re-layouts: 25.5 us -> 0.03 us  [pick(): got = jnp.where(chosen[:, f:f + 1], parts[f], got)]
    unnamed x7 -> x0, waiting for transfers between devices: 18.8 us -> none
  transfers between devices with their start and end apart: 9 -> 28, of which waited for: 9 -> 18; matrix products, arithmetic and copies ran while one was open for 4% -> 0% of each run, Pallas kernels for 0% -> 11%
where the time goes in v1:
time: 192 us; the launch traced here: 191 us
  waiting for transfers between devices  88.1 us (46%)
  Pallas kernels  42.8 us (22%)
  starting transfers between devices  31.2 us (16%)
  local copies, waits for them, and re-layouts  21.5 us (11%)
  other arithmetic  7.06 us (4%)
    ppermute x22, waiting for transfers between devices, swapped(): return lax.ppermute(x, axis, [(i, i ^ bit) for i in range(size)])  62.3 us
    pallas_call x22, Pallas kernels, call(): pl.pallas_call(kernel, out_shape=out_shape, in_specs=specs, out_specs=out...  42.8 us
    ppermute x6, waiting for transfers between devices, passed(): lax.ppermute(x, axis, [(i, (i + distance) % size) for i in range(size)])  25.7 us
    ppermute x22, starting transfers between devices, swapped(): return lax.ppermute(x, axis, [(i, i ^ bit) for i in range(size)])  22.1 us
    unnamed x12, local copies, waits for them, and re-layouts  21.5 us
    ppermute x6, starting transfers between devices, passed(): lax.ppermute(x, axis, [(i, (i + distance) % size) for i in range(size)])  9.18 us
  transfers between devices with their start and end apart: 28, of which 18 were waited for; matrix products, arithmetic and copies ran while one was open for 0% of the time, Pallas kernels for 11%

profile of v1, /device:TPU:0, one launch (start us, length us, event | category | flops | bytes accessed | tf_op | source)
XLA Modules:
  0.0 191.2 jit_solution(1741993447259641974)
XLA Ops:
  2.5 5.8 %copy-done.3 = bf16[1,2048,4096]{2,1,0:T(8,128)(2,1)S(1)} copy-done((bf16[1,2048,4096]{2,1,0:T(8,128)(2,1)S(1)}, bf16[1,2048,4096]{2,1,0:T(8,128)(2,1)}, u32[]{:S(2)}) %copy-start.3) | copy-done | bytes 16777240
  8.3 13.3 %load_and_project.1 = (bf16[2048,4096]{1,0:T(8,128)(2,1)S(1)}, f32[80,2048]{1,0:T(8,128)S(1)}) custom-call(bf16[2048,4096]{1,0:T(8,128)(2,1)S(1)} %bitcast.87, s32[16,32]{1,0:T(8,128)S(1)} %bitcast.88, bf16[80,4096]{1,0:T(8,128)(2,1)S(1)} %concatenate.9.volume), custom_call_target="tpu_custom_call" | custom-call | flops 1073741824 | bytes 16777216 | tf_op jit(solution)/shard_map/load_and_project/pallas_call | solution.py:21
  21.6 5.7 %copy-done = bf16[2048,4096]{1,0:T(8,128)(2,1)} copy-done((bf16[2048,4096]{1,0:T(8,128)(2,1)}, bf16[2048,4096]{1,0:T(8,128)(2,1)S(1)}, u32[]{:S(2)}) %copy-start) | copy-done | bytes 16777240
  29.0 3.0 %collective-permute-start.1 = (f16[80,1024]{1,0:T(8,128)(2,1)S(1)}, f16[80,1024]{1,0:T(8,128)(2,1)S(1)}, u32[]{:S(2)}, u32[]{:S(2)}) collective-permute-start(f16[80,1024]{1,0:T(8,128)(2,1)S(1)} %fusion.11), channel_id=1, source_target_pairs={{0,2},{1,3},{2,0},{3,1},{4,6},{5,7},{6,4},{7,5},{8,10},{9,11},{10,... | collective-permute-start | bytes 491528 | tf_op jit(solution)/shard_map/ppermute | solution.py:113
  32.0 4.5 %collective-permute-done.1 = f16[80,1024]{1,0:T(8,128)(2,1)S(1)} collective-permute-done((f16[80,1024]{1,0:T(8,128)(2,1)S(1)}, f16[80,1024]{1,0:T(8,128)(2,1)S(1)}, u32[]{:S(2)}, u32[]{:S(2)}) %collective-permute-start.1) | collective-permute-done | bytes 163872 | tf_op jit(solution)/shard_map/ppermute | solution.py:113
  36.6 2.8 %collective-permute-start.2 = (f16[80,1024]{1,0:T(8,128)(2,1)S(1)}, f16[80,1024]{1,0:T(8,128)(2,1)S(1)}, u32[]{:S(2)}, u32[]{:S(2)}) collective-permute-start(f16[80,1024]{1,0:T(8,128)(2,1)S(1)} %fusion.4), channel_id=1, source_target_pairs={{0,4},{1,5},{2,6},{3,7},{4,0},{5,1},{6,2},{7,3},{8,12},{9,13},{10,... | collective-permute-start | bytes 491528 | tf_op jit(solution)/shard_map/ppermute | solution.py:113
  39.4 7.4 %collective-permute-done.2 = f16[80,1024]{1,0:T(8,128)(2,1)S(1)} collective-permute-done((f16[80,1024]{1,0:T(8,128)(2,1)S(1)}, f16[80,1024]{1,0:T(8,128)(2,1)S(1)}, u32[]{:S(2)}, u32[]{:S(2)}) %collective-permute-start.2) | collective-permute-done | bytes 163872 | tf_op jit(solution)/shard_map/ppermute | solution.py:113
  47.4 5.8 %copy-done.1 = bf16[2048,4096]{1,0:T(8,128)(2,1)S(1)} copy-done((bf16[2048,4096]{1,0:T(8,128)(2,1)S(1)}, bf16[2048,4096]{1,0:T(8,128)(2,1)}, u32[]{:S(2)}) %copy-start.1) | copy-done | bytes 16777240
  54.7 4.2 %copy-done.2 = bf16[2048,4096]{1,0:T(8,128)(2,1)S(1)} copy-done((bf16[2048,4096]{1,0:T(8,128)(2,1)S(1)}, bf16[2048,4096]{1,0:T(8,128)(2,1)}, u32[]{:S(2)}) %copy-start.2) | copy-done | bytes 16777240
  63.7 6.2 %collective-permute-done.5 = f16[64,2048]{1,0:T(8,128)(2,1)S(1)} collective-permute-done((f16[64,2048]{1,0:T(8,128)(2,1)S(1)}, f16[64,2048]{1,0:T(8,128)(2,1)S(1)}, u32[]{:S(2)}, u32[]{:S(2)}) %collective-permute-start.5) | collective-permute-done | bytes 262176 | tf_op jit(solution)/shard_map/ppermute | solution.py:108
  70.0 2.6 %project_first.3.so_far = f32[64,2048]{1,0:T(8,128)S(1)} custom-call(bf16[64,2048]{1,0:T(8,128)(2,1)S(1)} %get-tuple-element.30.volume, bf16[2048,4096]{1,0:T(8,128)(2,1)S(1)} %copy-done.2), custom_call_target="tpu_custom_call" | custom-call | flops 536870912 | bytes 8388608 | tf_op jit(solution)/shard_map/project_first/pallas_call | solution.py:21
  72.6 2.5 %collective-permute-done.4 = f16[64,2048]{1,0:T(8,128)(2,1)S(1)} collective-permute-done((f16[64,2048]{1,0:T(8,128)(2,1)S(1)}, f16[64,2048]{1,0:T(8,128)(2,1)S(1)}, u32[]{:S(2)}, u32[]{:S(2)}) %collective-permute-start.4) | collective-permute-done | bytes 262176 | tf_op jit(solution)/shard_map/ppermute | solution.py:108
  78.7 5.4 %collective-permute-done.7 = f16[64,1024]{1,0:T(8,128)(2,1)S(1)} collective-permute-done((f16[64,1024]{1,0:T(8,128)(2,1)S(1)}, f16[64,1024]{1,0:T(8,128)(2,1)S(1)}, u32[]{:S(2)}, u32[]{:S(2)}) %collective-permute-start.7) | collective-permute-done | bytes 131104 | tf_op jit(solution)/shard_map/ppermute | solution.py:113
  84.2 2.2 %collective-permute-start.8 = (f16[64,1024]{1,0:T(8,128)(2,1)S(1)}, f16[64,1024]{1,0:T(8,128)(2,1)S(1)}, u32[]{:S(2)}, u32[]{:S(2)}) collective-permute-start(f16[64,1024]{1,0:T(8,128)(2,1)S(1)} %fusion.5), channel_id=1, source_target_pairs={{0,4},{1,5},{2,6},{3,7},{4,0},{5,1},{6,2},{7,3},{8,12},{9,13},{10,... | collective-permute-start | bytes 393224 | tf_op jit(solution)/shard_map/ppermute | solution.py:113
  86.4 6.7 %collective-permute-done.8 = f16[64,1024]{1,0:T(8,128)(2,1)S(1)} collective-permute-done((f16[64,1024]{1,0:T(8,128)(2,1)S(1)}, f16[64,1024]{1,0:T(8,128)(2,1)S(1)}, u32[]{:S(2)}, u32[]{:S(2)}) %collective-permute-start.8) | collective-permute-done | bytes 131104 | tf_op jit(solution)/shard_map/ppermute | solution.py:113
  97.3 2.6 %collective-permute-start.10 = (f16[64,2048]{1,0:T(8,128)(2,1)S(1)}, f16[64,2048]{1,0:T(8,128)(2,1)S(1)}, u32[]{:S(2)}, u32[]{:S(2)}) collective-permute-start(f16[64,2048]{1,0:T(8,128)(2,1)S(1)} %convert_element_type.188), channel_id=1, source_target_pairs={{0,8},{8,16},{16,24},{24,0},{1,9},{9,17},{17,25},{25,1},{2,10},{10... | collective-permute-start | bytes 786440 | tf_op jit(solution)/shard_map/ppermute | solution.py:108
  99.9 6.0 %collective-permute-done.11 = f16[64,2048]{1,0:T(8,128)(2,1)S(1)} collective-permute-done((f16[64,2048]{1,0:T(8,128)(2,1)S(1)}, f16[64,2048]{1,0:T(8,128)(2,1)S(1)}, u32[]{:S(2)}, u32[]{:S(2)}) %collective-permute-start.11) | collective-permute-done | bytes 262176 | tf_op jit(solution)/shard_map/ppermute | solution.py:108
  106.0 2.6 %project_first.4.so_far = f32[64,2048]{1,0:T(8,128)S(1)} custom-call(bf16[64,2048]{1,0:T(8,128)(2,1)S(1)} %get-tuple-element.26.volume, bf16[2048,4096]{1,0:T(8,128)(2,1)S(1)} %copy-done.2), custom_call_target="tpu_custom_call" | custom-call | flops 536870912 | bytes 8388608 | tf_op jit(solution)/shard_map/project_first/pallas_call | solution.py:21
  108.6 2.5 %collective-permute-done.10 = f16[64,2048]{1,0:T(8,128)(2,1)S(1)} collective-permute-done((f16[64,2048]{1,0:T(8,128)(2,1)S(1)}, f16[64,2048]{1,0:T(8,128)(2,1)S(1)}, u32[]{:S(2)}, u32[]{:S(2)}) %collective-permute-start.10) | collective-permute-done | bytes 262176 | tf_op jit(solution)/shard_map/ppermute | solution.py:108
  114.7 5.4 %collective-permute-done.13 = f16[64,1024]{1,0:T(8,128)(2,1)S(1)} collective-permute-done((f16[64,1024]{1,0:T(8,128)(2,1)S(1)}, f16[64,1024]{1,0:T(8,128)(2,1)S(1)}, u32[]{:S(2)}, u32[]{:S(2)}) %collective-permute-start.13) | collective-permute-done | bytes 131104 | tf_op jit(solution)/shard_map/ppermute | solution.py:113
  120.2 2.2 %collective-permute-start.14 = (f16[64,1024]{1,0:T(8,128)(2,1)S(1)}, f16[64,1024]{1,0:T(8,128)(2,1)S(1)}, u32[]{:S(2)}, u32[]{:S(2)}) collective-permute-start(f16[64,1024]{1,0:T(8,128)(2,1)S(1)} %fusion.6), channel_id=1, source_target_pairs={{0,4},{1,5},{2,6},{3,7},{4,0},{5,1},{6,2},{7,3},{8,12},{9,13},{10,... | collective-permute-start | bytes 393224 | tf_op jit(solution)/shard_map/ppermute | solution.py:113
  122.4 6.7 %collective-permute-done.14 = f16[64,1024]{1,0:T(8,128)(2,1)S(1)} collective-permute-done((f16[64,1024]{1,0:T(8,128)(2,1)S(1)}, f16[64,1024]{1,0:T(8,128)(2,1)S(1)}, u32[]{:S(2)}, u32[]{:S(2)}) %collective-permute-start.14) | collective-permute-done | bytes 131104 | tf_op jit(solution)/shard_map/ppermute | solution.py:113
  132.9 3.1 %collective-permute-start.16 = (f16[64,2048]{1,0:T(8,128)(2,1)S(1)}, f16[64,2048]{1,0:T(8,128)(2,1)S(1)}, u32[]{:S(2)}, u32[]{:S(2)}) collective-permute-start(f16[64,2048]{1,0:T(8,128)(2,1)S(1)} %convert_element_type.201), channel_id=1, source_target_pairs={{0,8},{8,16},{16,24},{24,0},{1,9},{9,17},{17,25},{25,1},{2,10},{10... | collective-permute-start | bytes 786440 | tf_op jit(solution)/shard_map/ppermute | solution.py:108
  136.0 6.0 %collective-permute-done.17 = f16[64,2048]{1,0:T(8,128)(2,1)S(1)} collective-permute-done((f16[64,2048]{1,0:T(8,128)(2,1)S(1)}, f16[64,2048]{1,0:T(8,128)(2,1)S(1)}, u32[]{:S(2)}, u32[]{:S(2)}) %collective-permute-start.17) | collective-permute-done | bytes 262176 | tf_op jit(solution)/shard_map/ppermute | solution.py:108
  142.0 2.6 %project_first.5.so_far = f32[64,2048]{1,0:T(8,128)S(1)} custom-call(bf16[64,2048]{1,0:T(8,128)(2,1)S(1)} %get-tuple-element.22.volume, bf16[2048,4096]{1,0:T(8,128)(2,1)S(1)} %copy-done.2), custom_call_target="tpu_custom_call" | custom-call | flops 536870912 | bytes 8388608 | tf_op jit(solution)/shard_map/project_first/pallas_call | solution.py:21
  144.7 2.5 %collective-permute-done.16 = f16[64,2048]{1,0:T(8,128)(2,1)S(1)} collective-permute-done((f16[64,2048]{1,0:T(8,128)(2,1)S(1)}, f16[64,2048]{1,0:T(8,128)(2,1)S(1)}, u32[]{:S(2)}, u32[]{:S(2)}) %collective-permute-start.16) | collective-permute-done | bytes 262176 | tf_op jit(solution)/shard_map/ppermute | solution.py:108
  150.6 5.5 %collective-permute-done.19 = f16[64,1024]{1,0:T(8,128)(2,1)S(1)} collective-permute-done((f16[64,1024]{1,0:T(8,128)(2,1)S(1)}, f16[64,1024]{1,0:T(8,128)(2,1)S(1)}, u32[]{:S(2)}, u32[]{:S(2)}) %collective-permute-start.19) | collective-permute-done | bytes 131104 | tf_op jit(solution)/shard_map/ppermute | solution.py:113
  156.2 2.1 %collective-permute-start.20 = (f16[64,1024]{1,0:T(8,128)(2,1)S(1)}, f16[64,1024]{1,0:T(8,128)(2,1)S(1)}, u32[]{:S(2)}, u32[]{:S(2)}) collective-permute-start(f16[64,1024]{1,0:T(8,128)(2,1)S(1)} %fusion.7), channel_id=1, source_target_pairs={{0,4},{1,5},{2,6},{3,7},{4,0},{5,1},{6,2},{7,3},{8,12},{9,13},{10,... | collective-permute-start | bytes 393224 | tf_op jit(solution)/shard_map/ppermute | solution.py:113
  158.3 6.8 %collective-permute-done.20 = f16[64,1024]{1,0:T(8,128)(2,1)S(1)} collective-permute-done((f16[64,1024]{1,0:T(8,128)(2,1)S(1)}, f16[64,1024]{1,0:T(8,128)(2,1)S(1)}, u32[]{:S(2)}, u32[]{:S(2)}) %collective-permute-start.20) | collective-permute-done | bytes 131104 | tf_op jit(solution)/shard_map/ppermute | solution.py:113
  173.0 4.1 %collective-permute-done.25 = bf16[64,2048]{1,0:T(8,128)(2,1)S(1)} collective-permute-done((bf16[64,2048]{1,0:T(8,128)(2,1)S(1)}, bf16[64,2048]{1,0:T(8,128)(2,1)S(1)}, u32[]{:S(2)}, u32[]{:S(2)}) %collective-permute-start.25) | collective-permute-done | bytes 262176 | tf_op jit(solution)/shard_map/ppermute | solution.py:113
  180.1 3.6 %collective-permute-done.27 = bf16[64,2048]{1,0:T(8,128)(2,1)S(1)} collective-permute-done((bf16[64,2048]{1,0:T(8,128)(2,1)S(1)}, bf16[64,2048]{1,0:T(8,128)(2,1)S(1)}, u32[]{:S(2)}, u32[]{:S(2)}) %collective-permute-start.27) | collective-permute-done | bytes 262176 | tf_op jit(solution)/shard_map/ppermute | solution.py:113
  183.7 5.2 %collective-permute-done.26 = bf16[64,2048]{1,0:T(8,128)(2,1)S(1)} collective-permute-done((bf16[64,2048]{1,0:T(8,128)(2,1)S(1)}, bf16[64,2048]{1,0:T(8,128)(2,1)S(1)}, u32[]{:S(2)}, u32[]{:S(2)}) %collective-permute-start.26) | collective-permute-done | bytes 262176 | tf_op jit(solution)/shard_map/ppermute | solution.py:113
  (103 shorter events, 43.0 us)
Async XLA Ops:
  2.5 5.8 %copy-start.3 = (bf16[1,2048,4096]{2,1,0:T(8,128)(2,1)S(1)}, bf16[1,2048,4096]{2,1,0:T(8,128)(2,1)}, u32[]{:S(2)}) copy-start(bf16[1,2048,4096]{2,1,0:T(8,128)(2,1)} %param.7) | copy-start | bytes 50331652
  27.3 19.6 %copy-start.5 = (bf16[1,4,64,2048]{3,2,1,0:T(8,128)(2,1)S(1)}, bf16[1,4,64,2048]{3,2,1,0:T(8,128)(2,1)}, u32[]{:S(2)}) copy-start(bf16[1,4,64,2048]{3,2,1,0:T(8,128)(2,1)} %param.6) | copy-start | bytes 3145732
  27.4 1.5 collective-permute-start
  29.0 7.5 %collective-permute-start.1 = (f16[80,1024]{1,0:T(8,128)(2,1)S(1)}, f16[80,1024]{1,0:T(8,128)(2,1)S(1)}, u32[]{:S(2)}, u32[]{:S(2)}) collective-permute-start(f16[80,1024]{1,0:T(8,128)(2,1)S(1)} %fusion.11), channel_id=1, source_target_pairs={{0,2},{1,3},{2,0},{3,1},{4,6},{5,7},{6,4},{7,5},{8,10},{9,11},{10,... | collective-permute-start | bytes 491528 | tf_op jit(solution)/shard_map/ppermute | solution.py:113
  36.6 10.2 %collective-permute-start.2 = (f16[80,1024]{1,0:T(8,128)(2,1)S(1)}, f16[80,1024]{1,0:T(8,128)(2,1)S(1)}, u32[]{:S(2)}, u32[]{:S(2)}) collective-permute-start(f16[80,1024]{1,0:T(8,128)(2,1)S(1)} %fusion.4), channel_id=1, source_target_pairs={{0,4},{1,5},{2,6},{3,7},{4,0},{5,1},{6,2},{7,3},{8,12},{9,13},{10,... | collective-permute-start | bytes 491528 | tf_op jit(solution)/shard_map/ppermute | solution.py:113
  47.2 7.5 %collective-permute-start.3 = (bf16[80,1024]{1,0:T(8,128)(2,1)S(1)}, bf16[80,1024]{1,0:T(8,128)(2,1)S(1)}, u32[]{:S(2)}, u32[]{:S(2)}) collective-permute-start(bf16[80,1024]{1,0:T(8,128)(2,1)S(1)} %concatenate.10.residue), channel_id=1, source_target_pairs={{0,1},{1,0},{2,3},{3,2},{4,5},{5,4},{6,7},{7,6},{8,9},{9,8},{10,11... | collective-permute-start | bytes 491528 | tf_op jit(solution)/shard_map/ppermute | solution.py:113
  47.4 5.8 %copy-start.1 = (bf16[2048,4096]{1,0:T(8,128)(2,1)S(1)}, bf16[2048,4096]{1,0:T(8,128)(2,1)}, u32[]{:S(2)}) copy-start(bf16[2048,4096]{1,0:T(8,128)(2,1)} %copy-done) | copy-start | bytes 50331652
  53.1 5.8 %copy-start.2 = (bf16[2048,4096]{1,0:T(8,128)(2,1)S(1)}, bf16[2048,4096]{1,0:T(8,128)(2,1)}, u32[]{:S(2)}) copy-start(bf16[2048,4096]{1,0:T(8,128)(2,1)} %copy-done) | copy-start | bytes 50331652
  59.8 10.1 %collective-permute-start.5 = (f16[64,2048]{1,0:T(8,128)(2,1)S(1)}, f16[64,2048]{1,0:T(8,128)(2,1)S(1)}, u32[]{:S(2)}, u32[]{:S(2)}) collective-permute-start(f16[64,2048]{1,0:T(8,128)(2,1)S(1)} %convert_element_type.178), channel_id=1, source_target_pairs={{0,8},{8,16},{16,24},{24,0},{1,9},{9,17},{17,25},{25,1},{2,10},{10... | collective-permute-start | bytes 786440 | tf_op jit(solution)/shard_map/ppermute | solution.py:108
  62.2 13.0 %collective-permute-start.4 = (f16[64,2048]{1,0:T(8,128)(2,1)S(1)}, f16[64,2048]{1,0:T(8,128)(2,1)S(1)}, u32[]{:S(2)}, u32[]{:S(2)}) collective-permute-start(f16[64,2048]{1,0:T(8,128)(2,1)S(1)} %convert_element_type.174), channel_id=1, source_target_pairs={{0,8},{8,16},{16,24},{24,0},{1,9},{9,17},{17,25},{25,1},{2,10},{10... | collective-permute-start | bytes 786440 | tf_op jit(solution)/shard_map/ppermute | solution.py:108
  76.6 1.5 collective-permute-start.6
  78.1 6.0 %collective-permute-start.7 = (f16[64,1024]{1,0:T(8,128)(2,1)S(1)}, f16[64,1024]{1,0:T(8,128)(2,1)S(1)}, u32[]{:S(2)}, u32[]{:S(2)}) collective-permute-start(f16[64,1024]{1,0:T(8,128)(2,1)S(1)} %fusion.8), channel_id=1, source_target_pairs={{0,2},{1,3},{2,0},{3,1},{4,6},{5,7},{6,4},{7,5},{8,10},{9,11},{10,... | collective-permute-start | bytes 393224 | tf_op jit(solution)/shard_map/ppermute | solution.py:113
  84.2 8.9 %collective-permute-start.8 = (f16[64,1024]{1,0:T(8,128)(2,1)S(1)}, f16[64,1024]{1,0:T(8,128)(2,1)S(1)}, u32[]{:S(2)}, u32[]{:S(2)}) collective-permute-start(f16[64,1024]{1,0:T(8,128)(2,1)S(1)} %fusion.5), channel_id=1, source_target_pairs={{0,4},{1,5},{2,6},{3,7},{4,0},{5,1},{6,2},{7,3},{8,12},{9,13},{10,... | collective-permute-start | bytes 393224 | tf_op jit(solution)/shard_map/ppermute | solution.py:113
  93.3 1.6 collective-permute-start.9
  95.9 10.1 %collective-permute-start.11 = (f16[64,2048]{1,0:T(8,128)(2,1)S(1)}, f16[64,2048]{1,0:T(8,128)(2,1)S(1)}, u32[]{:S(2)}, u32[]{:S(2)}) collective-permute-start(f16[64,2048]{1,0:T(8,128)(2,1)S(1)} %convert_element_type.191), channel_id=1, source_target_pairs={{0,8},{8,16},{16,24},{24,0},{1,9},{9,17},{17,25},{25,1},{2,10},{10... | collective-permute-start | bytes 786440 | tf_op jit(solution)/shard_map/ppermute | solution.py:108
  97.3 13.9 %collective-permute-start.10 = (f16[64,2048]{1,0:T(8,128)(2,1)S(1)}, f16[64,2048]{1,0:T(8,128)(2,1)S(1)}, u32[]{:S(2)}, u32[]{:S(2)}) collective-permute-start(f16[64,2048]{1,0:T(8,128)(2,1)S(1)} %convert_element_type.188), channel_id=1, source_target_pairs={{0,8},{8,16},{16,24},{24,0},{1,9},{9,17},{17,25},{25,1},{2,10},{10... | collective-permute-start | bytes 786440 | tf_op jit(solution)/shard_map/ppermute | solution.py:108
  112.6 1.5 collective-permute-start.12
  114.2 6.0 %collective-permute-start.13 = (f16[64,1024]{1,0:T(8,128)(2,1)S(1)}, f16[64,1024]{1,0:T(8,128)(2,1)S(1)}, u32[]{:S(2)}, u32[]{:S(2)}) collective-permute-start(f16[64,1024]{1,0:T(8,128)(2,1)S(1)} %fusion.9), channel_id=1, source_target_pairs={{0,2},{1,3},{2,0},{3,1},{4,6},{5,7},{6,4},{7,5},{8,10},{9,11},{10,... | collective-permute-start | bytes 393224 | tf_op jit(solution)/shard_map/ppermute | solution.py:113
  120.2 8.9 %collective-permute-start.14 = (f16[64,1024]{1,0:T(8,128)(2,1)S(1)}, f16[64,1024]{1,0:T(8,128)(2,1)S(1)}, u32[]{:S(2)}, u32[]{:S(2)}) collective-permute-start(f16[64,1024]{1,0:T(8,128)(2,1)S(1)} %fusion.6), channel_id=1, source_target_pairs={{0,4},{1,5},{2,6},{3,7},{4,0},{5,1},{6,2},{7,3},{8,12},{9,13},{10,... | collective-permute-start | bytes 393224 | tf_op jit(solution)/shard_map/ppermute | solution.py:113
  129.3 1.6 collective-permute-start.15
  131.9 10.1 %collective-permute-start.17 = (f16[64,2048]{1,0:T(8,128)(2,1)S(1)}, f16[64,2048]{1,0:T(8,128)(2,1)S(1)}, u32[]{:S(2)}, u32[]{:S(2)}) collective-permute-start(f16[64,2048]{1,0:T(8,128)(2,1)S(1)} %convert_element_type.204), channel_id=1, source_target_pairs={{0,8},{8,16},{16,24},{24,0},{1,9},{9,17},{17,25},{25,1},{2,10},{10... | collective-permute-start | bytes 786440 | tf_op jit(solution)/shard_map/ppermute | solution.py:108
  132.9 14.3 %collective-permute-start.16 = (f16[64,2048]{1,0:T(8,128)(2,1)S(1)}, f16[64,2048]{1,0:T(8,128)(2,1)S(1)}, u32[]{:S(2)}, u32[]{:S(2)}) collective-permute-start(f16[64,2048]{1,0:T(8,128)(2,1)S(1)} %convert_element_type.201), channel_id=1, source_target_pairs={{0,8},{8,16},{16,24},{24,0},{1,9},{9,17},{17,25},{25,1},{2,10},{10... | collective-permute-start | bytes 786440 | tf_op jit(solution)/shard_map/ppermute | solution.py:108
  148.7 1.5 collective-permute-start.18
  150.2 6.0 %collective-permute-start.19 = (f16[64,1024]{1,0:T(8,128)(2,1)S(1)}, f16[64,1024]{1,0:T(8,128)(2,1)S(1)}, u32[]{:S(2)}, u32[]{:S(2)}) collective-permute-start(f16[64,1024]{1,0:T(8,128)(2,1)S(1)} %fusion.10), channel_id=1, source_target_pairs={{0,2},{1,3},{2,0},{3,1},{4,6},{5,7},{6,4},{7,5},{8,10},{9,11},{10,... | collective-permute-start | bytes 393224 | tf_op jit(solution)/shard_map/ppermute | solution.py:113
  156.2 8.9 %collective-permute-start.20 = (f16[64,1024]{1,0:T(8,128)(2,1)S(1)}, f16[64,1024]{1,0:T(8,128)(2,1)S(1)}, u32[]{:S(2)}, u32[]{:S(2)}) collective-permute-start(f16[64,1024]{1,0:T(8,128)(2,1)S(1)} %fusion.7), channel_id=1, source_target_pairs={{0,4},{1,5},{2,6},{3,7},{4,0},{5,1},{6,2},{7,3},{8,12},{9,13},{10,... | collective-permute-start | bytes 393224 | tf_op jit(solution)/shard_map/ppermute | solution.py:113
  165.4 1.6 collective-permute-start.21
  167.9 9.2 %collective-permute-start.25 = (bf16[64,2048]{1,0:T(8,128)(2,1)S(1)}, bf16[64,2048]{1,0:T(8,128)(2,1)S(1)}, u32[]{:S(2)}, u32[]{:S(2)}) collective-permute-start(bf16[64,2048]{1,0:T(8,128)(2,1)S(1)} %convert_element_type.215), channel_id=1, source_target_pairs={{0,8},{8,0},{16,24},{24,16},{1,9},{9,1},{17,25},{25,17},{2,10},{10... | collective-permute-start | bytes 786440 | tf_op jit(solution)/shard_map/ppermute | solution.py:113
  168.9 9.6 %collective-permute-start.22 = (bf16[64,2048]{1,0:T(8,128)(2,1)S(1)}, bf16[64,2048]{1,0:T(8,128)(2,1)S(1)}, u32[]{:S(2)}, u32[]{:S(2)}) collective-permute-start(bf16[64,2048]{1,0:T(8,128)(2,1)S(1)} %convert_element_type.214), channel_id=1, source_target_pairs={{0,16},{8,24},{16,0},{24,8},{1,17},{9,25},{17,1},{25,9},{2,18},{10... | collective-permute-start | bytes 786440 | tf_op jit(solution)/shard_map/ppermute | solution.py:113
  170.3 13.4 %collective-permute-start.27 = (bf16[64,2048]{1,0:T(8,128)(2,1)S(1)}, bf16[64,2048]{1,0:T(8,128)(2,1)S(1)}, u32[]{:S(2)}, u32[]{:S(2)}) collective-permute-start(bf16[64,2048]{1,0:T(8,128)(2,1)S(1)} %convert_element_type.215), channel_id=1, source_target_pairs={{0,16},{8,24},{16,0},{24,8},{1,17},{9,25},{17,1},{25,9},{2,18},{10... | collective-permute-start | bytes 786440 | tf_op jit(solution)/shard_map/ppermute | solution.py:113
  171.0 12.7 %collective-permute-start.24 = (bf16[64,2048]{1,0:T(8,128)(2,1)S(1)}, bf16[64,2048]{1,0:T(8,128)(2,1)S(1)}, u32[]{:S(2)}, u32[]{:S(2)}) collective-permute-start(bf16[64,2048]{1,0:T(8,128)(2,1)S(1)} %convert_element_type.214), channel_id=1, source_target_pairs={{0,8},{8,0},{16,24},{24,16},{1,9},{9,1},{17,25},{25,17},{2,10},{10... | collective-permute-start | bytes 786440 | tf_op jit(solution)/shard_map/ppermute | solution.py:113
  177.1 11.8 %collective-permute-start.26 = (bf16[64,2048]{1,0:T(8,128)(2,1)S(1)}, bf16[64,2048]{1,0:T(8,128)(2,1)S(1)}, u32[]{:S(2)}, u32[]{:S(2)}) collective-permute-start(bf16[64,2048]{1,0:T(8,128)(2,1)S(1)} %collective-permute-done.25), channel_id=1, source_target_pairs={{0,16},{8,24},{16,0},{24,8},{1,17},{9,25},{17,1},{25,9},{2,18},{10... | collective-permute-start | bytes 786440 | tf_op jit(solution)/shard_map/ppermute | solution.py:113
  178.5 10.5 %collective-permute-start.23 = (bf16[64,2048]{1,0:T(8,128)(2,1)S(1)}, bf16[64,2048]{1,0:T(8,128)(2,1)S(1)}, u32[]{:S(2)}, u32[]{:S(2)}) collective-permute-start(bf16[64,2048]{1,0:T(8,128)(2,1)S(1)} %collective-permute-done.22), channel_id=1, source_target_pairs={{0,8},{8,0},{16,24},{24,16},{1,9},{9,1},{17,25},{25,17},{2,10},{10... | collective-permute-start | bytes 786440 | tf_op jit(solution)/shard_map/ppermute | solution.py:113
  (2 other events, 8.3 us)

commit v2 on v1

v2 whole, which is shorter than its diff:
```python
import functools

import jax
import jax.numpy as jnp
from jax import lax
from jax.experimental import pallas as pl
from jax.experimental.pallas import tpu as pltpu
from jax.sharding import PartitionSpec as P

F32, BF16, F16 = jnp.float32, jnp.bfloat16, jnp.float16
RAY_SCALE = 2.0**-14
EXTRA = 16
CHUNKS = 2
GROUPS = 2
VM = pl.BlockSpec(memory_space=pltpu.VMEM)
SM = pl.BlockSpec(memory_space=pltpu.SMEM)
HB = pl.BlockSpec(memory_space=pltpu.HBM)


def call(kernel, out_shape, args, specs, flops, name, scratch=(), vmem=8 << 20):
    out_specs = jax.tree.map(lambda _: VM, out_shape)
    return pl.pallas_call(
        kernel,
        out_shape=out_shape,
        in_specs=specs,
        out_specs=out_specs,
        scratch_shapes=scratch,
        name=name,
        cost_estimate=pl.CostEstimate(flops=flops, bytes_accessed=flops // 64, transcendentals=0),
        compiler_params=pltpu.CompilerParams(vmem_limit_bytes=vmem),
    )(*args)


def shaped(shape, dtype=F32):
    return jax.ShapeDtypeStruct(shape, dtype)


def dot_nt(a, b):
    return lax.dot_general(a, b, (((1,), (1,)), ((), ())), preferred_element_type=F32)


def dot_nn(a, b):
    return lax.dot_general(a, b, (((1,), (0,)), ((), ())), preferred_element_type=F32)


def load_kernel(
    place, matrix_hbm, pattern, order, start_hbm, matrix, narrow, volume, turn, apart, second,
    fronts, sems, start_sem,
):
    ray_blocks, col_blocks = pattern.shape
    ray_count, voxels = matrix.shape
    side = ray_count // ray_blocks
    loads = sems.shape[0]
    rows = ray_count // loads
    per_load = ray_blocks // loads
    slices = fronts.shape[1]
    owner, core, owners = place[0], place[1], place[2]

    def piece(i):
        where = pl.ds(i * rows, rows)
        return pltpu.make_async_copy(matrix_hbm.at[where], matrix.at[where], sems.at[i])

    first = pltpu.make_async_copy(start_hbm, fronts, start_sem)
    first.start()
    for i in range(loads):
        piece(i).start()
    second[...] = jnp.full(second.shape, core.astype(F32))
    later = owner - order[...]
    later = jnp.where(later < 0, later + owners, later)
    turn[...] = later
    last = order[...] + (owners - 1)
    last = jnp.where(last >= owners, last - owners, last)
    apart[...] = last ^ owner
    narrow[slices:, :] = jnp.ones((narrow.shape[0] - slices, voxels), BF16)
    first.wait()
    chosen = [later[:, f : f + 1] == 0 for f in range(1, fronts.shape[0])]
    step = 4 * side

    @pl.loop(0, voxels // step)
    def _(i):
        cols = pl.ds(pl.multiple_of(i * step, step), step)
        got = fronts[0, :, cols].astype(F32)
        for f, here in enumerate(chosen):
            got = jnp.where(here, fronts[f + 1, :, cols].astype(F32), got)
        volume[:, cols] = got
        narrow[:slices, cols] = got.astype(BF16)

    @pl.loop(0, loads)
    def _(i):
        piece(i).wait()
        for r in range(per_load):
            block_row = i * per_load + r
            where = pl.ds(pl.multiple_of(block_row * side, side), side)
            for c in range(col_blocks):

                @pl.when(pattern[block_row, c] == 0)
                def _():
                    matrix[where, c * side : (c + 1) * side] = jnp.zeros((side, side), BF16)


def project_first(chunk, volume, matrix, rays):
    width = volume.shape[1]
    rays[...] = dot_nt(volume[...], matrix[:, chunk * width : (chunk + 1) * width])


def project_next(chunk, volume, so_far, matrix, rays):
    width = volume.shape[1]
    rays[...] = so_far[...] + dot_nt(volume[...], matrix[:, chunk * width : (chunk + 1) * width])


def project_whole(place, volume, matrix, rays):
    count = rays.shape[1]
    where = pl.ds(pl.multiple_of(place[0] * count, count), count)
    rays[...] = dot_nt(volume[...], matrix[where, :])


def project_piece(place, volume, so_far, matrix, rays):
    width = volume.shape[1]
    count = rays.shape[1]
    where = pl.ds(pl.multiple_of(place[0] * count, count), count)
    rays[...] = so_far[:, where] + dot_nt(volume[...], matrix[where, matrix.shape[1] - width :])


def spread_pair(mine, theirs, residue, their_residue, matrix, spread):
    count = residue.shape[1]
    where = pl.ds(pl.multiple_of(mine[0] * count, count), count)
    also = pl.ds(pl.multiple_of(theirs[0] * count, count), count)
    step = matrix.shape[1] // 4
    for c in range(4):
        cols = slice(c * step, (c + 1) * step)
        spread[:, cols] = dot_nn(residue[...], matrix[where, cols]) + dot_nn(
            their_residue[...], matrix[also, cols]
        )


def spread_next(place, residue, so_far, matrix, spread):
    count = residue.shape[1]
    where = pl.ds(pl.multiple_of(place[0] * count, count), count)
    step = matrix.shape[1] // 4
    for c in range(4):
        cols = slice(c * step, (c + 1) * step)
        spread[:, cols] = so_far[:, cols] + dot_nn(residue[...], matrix[where, cols])


def spread_last(chunk, first, place, residue, so_far, volume, column, matrix, out, *column_out):
    count = residue.shape[1]
    slices, width = out.shape
    cols = slice(chunk * width, (chunk + 1) * width)
    where = pl.ds(pl.multiple_of(place[0] * count, count), count)
    total = so_far[:, cols] + dot_nn(residue[...], matrix[where, cols])
    if first:
        inverse = 1.0 / total[slices : slices + 1, :]
        column_out[0][...] = inverse
        prior = volume[:, cols]
    else:
        inverse = column[...]
        prior = volume[...]
    out[...] = prior + total[:slices] * inverse


def passed(x, axis, distance):
    size = lax.axis_size(axis)
    return lax.ppermute(x, axis, [(i, (i + distance) % size) for i in range(size)])


def swapped(x, axis, bit):
    size = lax.axis_size(axis)
    return lax.ppermute(x, axis, [(i, i ^ bit) for i in range(size)])


def tile_sum(own, received):
    total = own + received.astype(F32)
    bit = 2
    while bit < lax.axis_size("tile"):
        total = total + swapped(total.astype(F16), "tile", bit).astype(F32)
        bit *= 2
    return total


def from_all_owners(chunks):
    owners = lax.axis_size("subset")
    if owners == 4 and len(chunks) == 2:
        near = [swapped(c, "subset", 1) for c in chunks]
        far = [swapped(c, "subset", 2) for c in chunks]
        both = [swapped(far[0], "subset", 1), swapped(near[1], "subset", 2)]
        return [chunks, near, far, both]
    return [chunks] + [[swapped(c, "subset", d) for c in chunks] for d in range(1, owners)]


def body(start_volume, measured, system_values, block_pattern, subset_order):
    owner = lax.axis_index("subset")
    owners = lax.axis_size("subset")
    core = lax.axis_index("tile") % 2
    fronts, slices, voxels = start_volume.shape
    ray_count = measured.shape[-1]
    ray_blocks = block_pattern.shape[1]
    piece = ray_count // (2 * GROUPS)
    width = voxels // CHUNKS
    passes = owners
    loads = ray_blocks // 2
    work = 2 * slices * ray_count * voxels
    place = jnp.stack([owner, core, jnp.int32(owners)]).astype(jnp.int32)
    own = [jnp.reshape(2 * g + core, (1,)).astype(jnp.int32) for g in range(GROUPS)]
    other = [jnp.reshape(2 * g + 1 - core, (1,)).astype(jnp.int32) for g in range(GROUPS)]
    place, own, other = lax.optimization_barrier((place, own, other))
    rows = slices + EXTRA

    def pick(j, parts):
        got = parts[0]
        for f in range(1, fronts):
            got = jnp.where(turn[:, f : f + 1] == j, parts[f], got)
        return got

    hbm = pltpu.with_memory_space_constraint
    matrix, all_rows, volume, turn, apart, second = call(
        load_kernel,
        (
            pltpu.VMEM((ray_count, voxels), BF16),
            shaped((rows, voxels), BF16),
            shaped((slices, voxels)),
            shaped((slices, fronts), jnp.int32),
            shaped((slices, fronts), jnp.int32),
            shaped((1, piece)),
        ),
        (
            place, hbm(system_values[0], pltpu.HBM), block_pattern[0], subset_order,
            hbm(start_volume, pltpu.HBM),
        ),
        [SM, HB, SM, VM, HB],
        work,
        "load",
        scratch=[
            pltpu.VMEM((fronts, slices, voxels), BF16),
            pltpu.SemaphoreType.DMA((loads,)),
            pltpu.SemaphoreType.DMA,
        ],
        vmem=10 << 20,
    )
    matrix = pltpu.with_memory_space_constraint(matrix, pltpu.VMEM)
    volume = [volume] * CHUNKS
    column = [None] * CHUNKS
    inverse_row = [None] * GROUPS
    for j in range(passes):
        if j == 0:

            def project(where):
                return call(
                    project_whole, shaped((rows, piece)), (where, all_rows, matrix),
                    [SM, VM, VM], work // (2 * GROUPS), "project_whole",
                )

        else:
            narrow = [v.astype(BF16) for v in volume]
            so_far = call(
                functools.partial(project_first, 0), shaped((slices, ray_count)),
                (narrow[0], matrix), [VM, VM], work // CHUNKS, "project_first",
            )
            for c in range(1, CHUNKS - 1):
                so_far = call(
                    functools.partial(project_next, c), shaped((slices, ray_count)),
                    (narrow[c], so_far, matrix), [VM, VM, VM], work // CHUNKS, "project_next",
                )

            def project(where):
                return call(
                    project_piece, shaped((slices, piece)), (where, narrow[-1], so_far, matrix),
                    [SM, VM, VM, VM], work // (CHUNKS * 2 * GROUPS), "project_piece",
                )

        targets = [
            measured[0][:, :, 2 * g * piece : (2 * g + 2) * piece] for g in range(GROUPS)
        ]
        targets = [
            jnp.where(second == 0, t[:, :, :piece], t[:, :, piece:]).astype(F32) for t in targets
        ]
        residues = []
        for g in range(GROUPS):
            sent = project(other[g])
            received = swapped((sent * RAY_SCALE).astype(F16), "tile", 1)
            held = project(own[g])
            total = tile_sum(held * RAY_SCALE, received)
            if j == 0:
                inverse_row[g] = 1.0 / total[slices : slices + 1]
                total = total[:slices]
            target = pick(j, targets[g]) * RAY_SCALE
            residue = ((target - total) * inverse_row[g]).astype(BF16)
            if j == 0:
                residue = jnp.concatenate([residue, jnp.ones((EXTRA, piece), BF16)])
            residues.append((residue, swapped(residue, "tile", 1)))
        height = residues[0][0].shape[0]
        for g in range(GROUPS - 1):
            if g == 0:
                spread = call(
                    spread_pair, shaped((height, voxels)),
                    (own[g], other[g], *residues[g], matrix), [SM, SM, VM, VM, VM],
                    work // GROUPS, "spread_pair",
                )
        spread = call(
            spread_next, shaped((height, voxels)), (own[-1], residues[-1][0], spread, matrix),
            [SM, VM, VM, VM], work // (2 * GROUPS), "spread_next",
        )
        for c in range(CHUNKS):
            shapes = [shaped((slices, width))]
            if j == 0:
                shapes.append(shaped((1, width)))
                prior = jnp.zeros((1, width), F32)
            else:
                prior = column[c]
            got = call(
                functools.partial(spread_last, c, j == 0), tuple(shapes),
                (other[-1], residues[-1][1], spread, volume[c], prior, matrix),
                [SM, VM, VM, VM, VM, VM], work // (2 * GROUPS * CHUNKS), "spread_last",
            )
            volume[c] = got[0]
            if j == 0:
                column[c] = got[1]
        if j + 1 < passes:
            volume = [passed(v.astype(F16), "subset", 1).astype(F32) for v in volume]

    found = from_all_owners([v.astype(BF16) for v in volume])
    outs = []
    for f in range(fronts):
        parts = []
        for c in range(CHUNKS):
            got = found[0][c]
            for d in range(1, owners):
                got = jnp.where(apart[:, f : f + 1] == d, found[d][c], got)
            parts.append(got)
        outs.append(jnp.concatenate(parts, axis=1))
    return jnp.stack(outs)


def solution(mesh):
    placed = (
        P(None, None, "tile"),
        P("subset", None, None, None),
        P("subset", None, "tile"),
        P("subset", None, "tile"),
        P(),
    )
    return jax.shard_map(
        body, mesh=mesh, in_specs=placed, out_specs=P(None, None, "tile"), check_vma=False
    )
```

time: 192 us -> 172 us (0.90)
  local copies, waits for them, and re-layouts: 21.5 us -> 1.5 us
  waiting for transfers between devices: 88.1 us -> 71.4 us
  starting transfers between devices: 31.2 us -> 43.8 us
  Pallas kernels: 42.8 us -> 49.1 us
    unnamed x12 -> x5, local copies, waits for them, and re-layouts: 21.5 us -> 1.47 us
    ppermute x22 -> x38, waiting for transfers between devices: 62.3 us -> 46.4 us  [swapped(): return lax.ppermute(x, axis, [(i, i ^ bit) for i in range(size)])]
    ppermute x22 -> x38, starting transfers between devices: 22.1 us -> 33.8 us  [swapped(): return lax.ppermute(x, axis, [(i, i ^ bit) for i in range(size)])]
    pallas_call x22 -> x36, Pallas kernels: 42.8 us -> 49.1 us  [call(): pl.pallas_call(kernel, out_shape=out_shape, in_specs=specs, out_specs=out...]
    select_n x2, other arithmetic: 2.47 us -> 0.53 us  [body(): got = jnp.where(apart[:, f:f + 1] == d, found[d][c], got)]
  transfers between devices with their start and end apart: 28 -> 44, of which waited for: 18 -> 26; matrix products, arithmetic and copies ran while one was open for 0% -> 2% of each run, Pallas kernels for 11% -> 17%
where the time goes in v2:
time: 172 us
  waiting for transfers between devices  71.4 us (42%)
  Pallas kernels  49.1 us (29%)
  starting transfers between devices  43.8 us (25%)
  other arithmetic  5.32 us (3%)
    pallas_call x36, Pallas kernels, call(): pl.pallas_call(kernel, out_shape=out_shape, in_specs=specs, out_specs=out...  49.1 us
    ppermute x38, waiting for transfers between devices, swapped(): return lax.ppermute(x, axis, [(i, i ^ bit) for i in range(size)])  46.4 us
    ppermute x38, starting transfers between devices, swapped(): return lax.ppermute(x, axis, [(i, i ^ bit) for i in range(size)])  33.8 us
    ppermute x6, waiting for transfers between devices, passed(): lax.ppermute(x, axis, [(i, (i + distance) % size) for i in range(size)])  25 us
    ppermute x6, starting transfers between devices, passed(): lax.ppermute(x, axis, [(i, (i + distance) % size) for i in range(size)])  10 us
  transfers between devices with their start and end apart: 44, of which 26 were waited for; matrix products, arithmetic and copies ran while one was open for 2% of the time, Pallas kernels for 17%

profile of v2, /device:TPU:0, one launch (start us, length us, event | category | flops | bytes accessed | tf_op | source)
XLA Modules:
  0.0 171.8 jit_solution(13064683471496672812)
XLA Ops:
  1.5 12.5 %load.1 = (bf16[2048,4096]{1,0:T(8,128)(2,1)S(1)}, bf16[80,4096]{1,0:T(8,128)(2,1)S(1)}, f32[64,4096]{1,0:T(8,128)S(1)}, s32[64,4]{1,0:T(8,128)S(1)}, s32[64,4]{1,0:T(8,128)S(1)}, /*index=5*/f32[1,512]{1,0:T(1,128)S(1)}) custom-call(s32[3]{0:T(128)S(1)} %pad_add_fusion.place, bf16[2048,4096]{1,0:T(8,128)(2,1)} %bitcast.99, s32[16,32]{1,0:T(8,128)S(1)} %bitcast.98, ...), custom_call_target="tpu_custom_call" | custom-call | flops 1073741824 | bytes 16777216 | tf_op jit(solution)/shard_map/load/pallas_call | solution.py:22
  20.9 3.1 %collective-permute-start.5 = (f16[80,512]{1,0:T(8,128)(2,1)S(1)}, f16[80,512]{1,0:T(8,128)(2,1)S(1)}, u32[]{:S(2)}, u32[]{:S(2)}) collective-permute-start(f16[80,512]{1,0:T(8,128)(2,1)S(1)} %fusion.15), channel_id=1, source_target_pairs={{0,2},{1,3},{2,0},{3,1},{4,6},{5,7},{6,4},{7,5},{8,10},{9,11},{10,... | collective-permute-start | bytes 245768 | tf_op jit(solution)/shard_map/ppermute | solution.py:168
  24.2 2.7 %collective-permute-done.5 = f16[80,512]{1,0:T(8,128)(2,1)S(1)} collective-permute-done((f16[80,512]{1,0:T(8,128)(2,1)S(1)}, f16[80,512]{1,0:T(8,128)(2,1)S(1)}, u32[]{:S(2)}, u32[]{:S(2)}) %collective-permute-start.5) | collective-permute-done | bytes 81952 | tf_op jit(solution)/shard_map/ppermute | solution.py:168
  26.9 3.2 %collective-permute-start.6 = (f16[80,512]{1,0:T(8,128)(2,1)S(1)}, f16[80,512]{1,0:T(8,128)(2,1)S(1)}, u32[]{:S(2)}, u32[]{:S(2)}) collective-permute-start(f16[80,512]{1,0:T(8,128)(2,1)S(1)} %fusion.7), channel_id=1, source_target_pairs={{0,4},{1,5},{2,6},{3,7},{4,0},{5,1},{6,2},{7,3},{8,12},{9,13},{10,... | collective-permute-start | bytes 245768 | tf_op jit(solution)/shard_map/ppermute | solution.py:168
  31.7 3.4 %collective-permute-done.6 = f16[80,512]{1,0:T(8,128)(2,1)S(1)} collective-permute-done((f16[80,512]{1,0:T(8,128)(2,1)S(1)}, f16[80,512]{1,0:T(8,128)(2,1)S(1)}, u32[]{:S(2)}, u32[]{:S(2)}) %collective-permute-start.6) | collective-permute-done | bytes 81952 | tf_op jit(solution)/shard_map/ppermute | solution.py:168
  35.2 1.8 %collective-permute-done.2 = f16[80,512]{1,0:T(8,128)(2,1)S(1)} collective-permute-done((f16[80,512]{1,0:T(8,128)(2,1)S(1)}, f16[80,512]{1,0:T(8,128)(2,1)S(1)}, u32[]{:S(2)}, u32[]{:S(2)}) %collective-permute-start.2) | collective-permute-done | bytes 81952 | tf_op jit(solution)/shard_map/ppermute | solution.py:168
  43.8 1.7 %collective-permute-start.8 = (f16[64,2048]{1,0:T(8,128)(2,1)S(1)}, f16[64,2048]{1,0:T(8,128)(2,1)S(1)}, u32[]{:S(2)}, u32[]{:S(2)}) collective-permute-start(f16[64,2048]{1,0:T(8,128)(2,1)S(1)} %convert_element_type.256), channel_id=1, source_target_pairs={{0,8},{8,16},{16,24},{24,0},{1,9},{9,17},{17,25},{25,1},{2,10},{10... | collective-permute-start | bytes 786440 | tf_op jit(solution)/shard_map/ppermute | solution.py:163
  45.6 6.2 %collective-permute-done.9 = f16[64,2048]{1,0:T(8,128)(2,1)S(1)} collective-permute-done((f16[64,2048]{1,0:T(8,128)(2,1)S(1)}, f16[64,2048]{1,0:T(8,128)(2,1)S(1)}, u32[]{:S(2)}, u32[]{:S(2)}) %collective-permute-start.9) | collective-permute-done | bytes 262176 | tf_op jit(solution)/shard_map/ppermute | solution.py:163
  51.8 2.6 %project_first.3.so_far = f32[64,2048]{1,0:T(8,128)S(1)} custom-call(bf16[64,2048]{1,0:T(8,128)(2,1)S(1)} %get-tuple-element.78.volume, bf16[2048,4096]{1,0:T(8,128)(2,1)S(1)} %get-tuple-element.27.matrix), custom_call_target="tpu_custom_call" | custom-call | flops 536870912 | bytes 8388608 | tf_op jit(solution)/shard_map/project_first/pallas_call | solution.py:22
  54.5 2.1 %collective-permute-done.8 = f16[64,2048]{1,0:T(8,128)(2,1)S(1)} collective-permute-done((f16[64,2048]{1,0:T(8,128)(2,1)S(1)}, f16[64,2048]{1,0:T(8,128)(2,1)S(1)}, u32[]{:S(2)}, u32[]{:S(2)}) %collective-permute-start.8) | collective-permute-done | bytes 262176 | tf_op jit(solution)/shard_map/ppermute | solution.py:163
  62.6 2.6 %collective-permute-done.15 = f16[64,512]{1,0:T(8,128)(2,1)S(1)} collective-permute-done((f16[64,512]{1,0:T(8,128)(2,1)S(1)}, f16[64,512]{1,0:T(8,128)(2,1)S(1)}, u32[]{:S(2)}, u32[]{:S(2)}) %collective-permute-start.15) | collective-permute-done | bytes 65568 | tf_op jit(solution)/shard_map/ppermute | solution.py:168
  66.7 2.4 %collective-permute-start.12 = (f16[64,512]{1,0:T(8,128)(2,1)S(1)}, f16[64,512]{1,0:T(8,128)(2,1)S(1)}, u32[]{:S(2)}, u32[]{:S(2)}) collective-permute-start(f16[64,512]{1,0:T(8,128)(2,1)S(1)} %fusion.8), channel_id=1, source_target_pairs={{0,4},{1,5},{2,6},{3,7},{4,0},{5,1},{6,2},{7,3},{8,12},{9,13},{10,... | collective-permute-start | bytes 196616 | tf_op jit(solution)/shard_map/ppermute | solution.py:168
  69.1 3.2 %collective-permute-done.16 = f16[64,512]{1,0:T(8,128)(2,1)S(1)} collective-permute-done((f16[64,512]{1,0:T(8,128)(2,1)S(1)}, f16[64,512]{1,0:T(8,128)(2,1)S(1)}, u32[]{:S(2)}, u32[]{:S(2)}) %collective-permute-start.16) | collective-permute-done | bytes 65568 | tf_op jit(solution)/shard_map/ppermute | solution.py:168
  77.9 2.7 %collective-permute-start.18 = (f16[64,2048]{1,0:T(8,128)(2,1)S(1)}, f16[64,2048]{1,0:T(8,128)(2,1)S(1)}, u32[]{:S(2)}, u32[]{:S(2)}) collective-permute-start(f16[64,2048]{1,0:T(8,128)(2,1)S(1)} %convert_element_type.276), channel_id=1, source_target_pairs={{0,8},{8,16},{16,24},{24,0},{1,9},{9,17},{17,25},{25,1},{2,10},{10... | collective-permute-start | bytes 786440 | tf_op jit(solution)/shard_map/ppermute | solution.py:163
  80.6 6.2 %collective-permute-done.19 = f16[64,2048]{1,0:T(8,128)(2,1)S(1)} collective-permute-done((f16[64,2048]{1,0:T(8,128)(2,1)S(1)}, f16[64,2048]{1,0:T(8,128)(2,1)S(1)}, u32[]{:S(2)}, u32[]{:S(2)}) %collective-permute-start.19) | collective-permute-done | bytes 262176 | tf_op jit(solution)/shard_map/ppermute | solution.py:163
  86.9 2.6 %project_first.4.so_far = f32[64,2048]{1,0:T(8,128)S(1)} custom-call(bf16[64,2048]{1,0:T(8,128)(2,1)S(1)} %get-tuple-element.74.volume, bf16[2048,4096]{1,0:T(8,128)(2,1)S(1)} %get-tuple-element.27.matrix), custom_call_target="tpu_custom_call" | custom-call | flops 536870912 | bytes 8388608 | tf_op jit(solution)/shard_map/project_first/pallas_call | solution.py:22
  89.5 2.1 %collective-permute-done.18 = f16[64,2048]{1,0:T(8,128)(2,1)S(1)} collective-permute-done((f16[64,2048]{1,0:T(8,128)(2,1)S(1)}, f16[64,2048]{1,0:T(8,128)(2,1)S(1)}, u32[]{:S(2)}, u32[]{:S(2)}) %collective-permute-start.18) | collective-permute-done | bytes 262176 | tf_op jit(solution)/shard_map/ppermute | solution.py:163
  97.7 2.8 %collective-permute-done.25 = f16[64,512]{1,0:T(8,128)(2,1)S(1)} collective-permute-done((f16[64,512]{1,0:T(8,128)(2,1)S(1)}, f16[64,512]{1,0:T(8,128)(2,1)S(1)}, u32[]{:S(2)}, u32[]{:S(2)}) %collective-permute-start.25) | collective-permute-done | bytes 65568 | tf_op jit(solution)/shard_map/ppermute | solution.py:168
  101.6 2.1 %collective-permute-start.22 = (f16[64,512]{1,0:T(8,128)(2,1)S(1)}, f16[64,512]{1,0:T(8,128)(2,1)S(1)}, u32[]{:S(2)}, u32[]{:S(2)}) collective-permute-start(f16[64,512]{1,0:T(8,128)(2,1)S(1)} %fusion.10), channel_id=1, source_target_pairs={{0,4},{1,5},{2,6},{3,7},{4,0},{5,1},{6,2},{7,3},{8,12},{9,13},{10,... | collective-permute-start | bytes 196616 | tf_op jit(solution)/shard_map/ppermute | solution.py:168
  103.7 3.5 %collective-permute-done.26 = f16[64,512]{1,0:T(8,128)(2,1)S(1)} collective-permute-done((f16[64,512]{1,0:T(8,128)(2,1)S(1)}, f16[64,512]{1,0:T(8,128)(2,1)S(1)}, u32[]{:S(2)}, u32[]{:S(2)}) %collective-permute-start.26) | collective-permute-done | bytes 65568 | tf_op jit(solution)/shard_map/ppermute | solution.py:168
  112.2 3.3 %collective-permute-start.28 = (f16[64,2048]{1,0:T(8,128)(2,1)S(1)}, f16[64,2048]{1,0:T(8,128)(2,1)S(1)}, u32[]{:S(2)}, u32[]{:S(2)}) collective-permute-start(f16[64,2048]{1,0:T(8,128)(2,1)S(1)} %convert_element_type.296), channel_id=1, source_target_pairs={{0,8},{8,16},{16,24},{24,0},{1,9},{9,17},{17,25},{25,1},{2,10},{10... | collective-permute-start | bytes 786440 | tf_op jit(solution)/shard_map/ppermute | solution.py:163
  115.5 6.2 %collective-permute-done.29 = f16[64,2048]{1,0:T(8,128)(2,1)S(1)} collective-permute-done((f16[64,2048]{1,0:T(8,128)(2,1)S(1)}, f16[64,2048]{1,0:T(8,128)(2,1)S(1)}, u32[]{:S(2)}, u32[]{:S(2)}) %collective-permute-start.29) | collective-permute-done | bytes 262176 | tf_op jit(solution)/shard_map/ppermute | solution.py:163
  121.8 2.7 %project_first.5.so_far = f32[64,2048]{1,0:T(8,128)S(1)} custom-call(bf16[64,2048]{1,0:T(8,128)(2,1)S(1)} %get-tuple-element.70.volume, bf16[2048,4096]{1,0:T(8,128)(2,1)S(1)} %get-tuple-element.27.matrix), custom_call_target="tpu_custom_call" | custom-call | flops 536870912 | bytes 8388608 | tf_op jit(solution)/shard_map/project_first/pallas_call | solution.py:22
  124.4 2.1 %collective-permute-done.28 = f16[64,2048]{1,0:T(8,128)(2,1)S(1)} collective-permute-done((f16[64,2048]{1,0:T(8,128)(2,1)S(1)}, f16[64,2048]{1,0:T(8,128)(2,1)S(1)}, u32[]{:S(2)}, u32[]{:S(2)}) %collective-permute-start.28) | collective-permute-done | bytes 262176 | tf_op jit(solution)/shard_map/ppermute | solution.py:163
  132.6 2.8 %collective-permute-done.35 = f16[64,512]{1,0:T(8,128)(2,1)S(1)} collective-permute-done((f16[64,512]{1,0:T(8,128)(2,1)S(1)}, f16[64,512]{1,0:T(8,128)(2,1)S(1)}, u32[]{:S(2)}, u32[]{:S(2)}) %collective-permute-start.35) | collective-permute-done | bytes 65568 | tf_op jit(solution)/shard_map/ppermute | solution.py:168
  136.5 2.1 %collective-permute-start.32 = (f16[64,512]{1,0:T(8,128)(2,1)S(1)}, f16[64,512]{1,0:T(8,128)(2,1)S(1)}, u32[]{:S(2)}, u32[]{:S(2)}) collective-permute-start(f16[64,512]{1,0:T(8,128)(2,1)S(1)} %fusion.12), channel_id=1, source_target_pairs={{0,4},{1,5},{2,6},{3,7},{4,0},{5,1},{6,2},{7,3},{8,12},{9,13},{10,... | collective-permute-start | bytes 196616 | tf_op jit(solution)/shard_map/ppermute | solution.py:168
  138.6 3.5 %collective-permute-done.36 = f16[64,512]{1,0:T(8,128)(2,1)S(1)} collective-permute-done((f16[64,512]{1,0:T(8,128)(2,1)S(1)}, f16[64,512]{1,0:T(8,128)(2,1)S(1)}, u32[]{:S(2)}, u32[]{:S(2)}) %collective-permute-start.36) | collective-permute-done | bytes 65568 | tf_op jit(solution)/shard_map/ppermute | solution.py:168
  149.2 5.7 %collective-permute-done.41 = bf16[64,2048]{1,0:T(8,128)(2,1)S(1)} collective-permute-done((bf16[64,2048]{1,0:T(8,128)(2,1)S(1)}, bf16[64,2048]{1,0:T(8,128)(2,1)S(1)}, u32[]{:S(2)}, u32[]{:S(2)}) %collective-permute-start.41) | collective-permute-done | bytes 262176 | tf_op jit(solution)/shard_map/ppermute | solution.py:168
  157.2 1.7 %collective-permute-start.39 = (bf16[64,2048]{1,0:T(8,128)(2,1)S(1)}, bf16[64,2048]{1,0:T(8,128)(2,1)S(1)}, u32[]{:S(2)}, u32[]{:S(2)}) collective-permute-start(bf16[64,2048]{1,0:T(8,128)(2,1)S(1)} %collective-permute-done.38), channel_id=1, source_target_pairs={{0,8},{8,0},{16,24},{24,16},{1,9},{9,1},{17,25},{25,17},{2,10},{10... | collective-permute-start | bytes 786440 | tf_op jit(solution)/shard_map/ppermute | solution.py:168
  158.9 3.0 %collective-permute-done.43 = bf16[64,2048]{1,0:T(8,128)(2,1)S(1)} collective-permute-done((bf16[64,2048]{1,0:T(8,128)(2,1)S(1)}, bf16[64,2048]{1,0:T(8,128)(2,1)S(1)}, u32[]{:S(2)}, u32[]{:S(2)}) %collective-permute-start.43) | collective-permute-done | bytes 262176 | tf_op jit(solution)/shard_map/ppermute | solution.py:168
  162.0 4.8 %collective-permute-done.42 = bf16[64,2048]{1,0:T(8,128)(2,1)S(1)} collective-permute-done((bf16[64,2048]{1,0:T(8,128)(2,1)S(1)}, bf16[64,2048]{1,0:T(8,128)(2,1)S(1)}, u32[]{:S(2)}, u32[]{:S(2)}) %collective-permute-start.42) | collective-permute-done | bytes 262176 | tf_op jit(solution)/shard_map/ppermute | solution.py:168
  167.1 2.7 %collective-permute-done.39 = bf16[64,2048]{1,0:T(8,128)(2,1)S(1)} collective-permute-done((bf16[64,2048]{1,0:T(8,128)(2,1)S(1)}, bf16[64,2048]{1,0:T(8,128)(2,1)S(1)}, u32[]{:S(2)}, u32[]{:S(2)}) %collective-permute-start.39) | collective-permute-done | bytes 262176 | tf_op jit(solution)/shard_map/ppermute | solution.py:168
  (159 shorter events, 60.8 us)
Async XLA Ops:
  15.5 5.4 %collective-permute-start.4 = (f16[80,512]{1,0:T(8,128)(2,1)S(1)}, f16[80,512]{1,0:T(8,128)(2,1)S(1)}, u32[]{:S(2)}, u32[]{:S(2)}) collective-permute-start(f16[80,512]{1,0:T(8,128)(2,1)S(1)} %multiply_convert_fusion), channel_id=1, source_target_pairs={{0,1},{1,0},{2,3},{3,2},{4,5},{5,4},{6,7},{7,6},{8,9},{9,8},{10,11... | collective-permute-start | bytes 245768 | tf_op jit(solution)/shard_map/ppermute | solution.py:168
  17.5 6.6 %collective-permute-start = (f16[80,512]{1,0:T(8,128)(2,1)S(1)}, f16[80,512]{1,0:T(8,128)(2,1)S(1)}, u32[]{:S(2)}, u32[]{:S(2)}) collective-permute-start(f16[80,512]{1,0:T(8,128)(2,1)S(1)} %multiply_convert_fusion.1), channel_id=1, source_target_pairs={{0,1},{1,0},{2,3},{3,2},{4,5},{5,4},{6,7},{7,6},{8,9},{9,8},{10,11... | collective-permute-start | bytes 245768 | tf_op jit(solution)/shard_map/ppermute | solution.py:168
  20.9 6.0 %collective-permute-start.5 = (f16[80,512]{1,0:T(8,128)(2,1)S(1)}, f16[80,512]{1,0:T(8,128)(2,1)S(1)}, u32[]{:S(2)}, u32[]{:S(2)}) collective-permute-start(f16[80,512]{1,0:T(8,128)(2,1)S(1)} %fusion.15), channel_id=1, source_target_pairs={{0,2},{1,3},{2,0},{3,1},{4,6},{5,7},{6,4},{7,5},{8,10},{9,11},{10,... | collective-permute-start | bytes 245768 | tf_op jit(solution)/shard_map/ppermute | solution.py:168
  24.1 6.1 %collective-permute-start.1 = (f16[80,512]{1,0:T(8,128)(2,1)S(1)}, f16[80,512]{1,0:T(8,128)(2,1)S(1)}, u32[]{:S(2)}, u32[]{:S(2)}) collective-permute-start(f16[80,512]{1,0:T(8,128)(2,1)S(1)} %fusion.14), channel_id=1, source_target_pairs={{0,2},{1,3},{2,0},{3,1},{4,6},{5,7},{6,4},{7,5},{8,10},{9,11},{10,... | collective-permute-start | bytes 245768 | tf_op jit(solution)/shard_map/ppermute | solution.py:168
  26.9 8.2 %collective-permute-start.6 = (f16[80,512]{1,0:T(8,128)(2,1)S(1)}, f16[80,512]{1,0:T(8,128)(2,1)S(1)}, u32[]{:S(2)}, u32[]{:S(2)}) collective-permute-start(f16[80,512]{1,0:T(8,128)(2,1)S(1)} %fusion.7), channel_id=1, source_target_pairs={{0,4},{1,5},{2,6},{3,7},{4,0},{5,1},{6,2},{7,3},{8,12},{9,13},{10,... | collective-permute-start | bytes 245768 | tf_op jit(solution)/shard_map/ppermute | solution.py:168
  30.2 6.8 %collective-permute-start.2 = (f16[80,512]{1,0:T(8,128)(2,1)S(1)}, f16[80,512]{1,0:T(8,128)(2,1)S(1)}, u32[]{:S(2)}, u32[]{:S(2)}) collective-permute-start(f16[80,512]{1,0:T(8,128)(2,1)S(1)} %fusion.6), channel_id=1, source_target_pairs={{0,4},{1,5},{2,6},{3,7},{4,0},{5,1},{6,2},{7,3},{8,12},{9,13},{10,... | collective-permute-start | bytes 245768 | tf_op jit(solution)/shard_map/ppermute | solution.py:168
  37.3 3.8 %collective-permute-start.3 = (bf16[80,512]{1,0:T(8,128)(2,1)S(1)}, bf16[80,512]{1,0:T(8,128)(2,1)S(1)}, u32[]{:S(2)}, u32[]{:S(2)}) collective-permute-start(bf16[80,512]{1,0:T(8,128)(2,1)S(1)} %concatenate.18.residue), channel_id=1, source_target_pairs={{0,1},{1,0},{2,3},{3,2},{4,5},{5,4},{6,7},{7,6},{8,9},{9,8},{10,11... | collective-permute-start | bytes 245768 | tf_op jit(solution)/shard_map/ppermute | solution.py:168
  41.7 10.1 %collective-permute-start.9 = (f16[64,2048]{1,0:T(8,128)(2,1)S(1)}, f16[64,2048]{1,0:T(8,128)(2,1)S(1)}, u32[]{:S(2)}, u32[]{:S(2)}) collective-permute-start(f16[64,2048]{1,0:T(8,128)(2,1)S(1)} %convert_element_type.259), channel_id=1, source_target_pairs={{0,8},{8,16},{16,24},{24,0},{1,9},{9,17},{17,25},{25,1},{2,10},{10... | collective-permute-start | bytes 786440 | tf_op jit(solution)/shard_map/ppermute | solution.py:163
  43.8 12.8 %collective-permute-start.8 = (f16[64,2048]{1,0:T(8,128)(2,1)S(1)}, f16[64,2048]{1,0:T(8,128)(2,1)S(1)}, u32[]{:S(2)}, u32[]{:S(2)}) collective-permute-start(f16[64,2048]{1,0:T(8,128)(2,1)S(1)} %convert_element_type.256), channel_id=1, source_target_pairs={{0,8},{8,16},{16,24},{24,0},{1,9},{9,17},{17,25},{25,1},{2,10},{10... | collective-permute-start | bytes 786440 | tf_op jit(solution)/shard_map/ppermute | solution.py:163
  60.4 4.8 %collective-permute-start.15 = (f16[64,512]{1,0:T(8,128)(2,1)S(1)}, f16[64,512]{1,0:T(8,128)(2,1)S(1)}, u32[]{:S(2)}, u32[]{:S(2)}) collective-permute-start(f16[64,512]{1,0:T(8,128)(2,1)S(1)} %fusion.17), channel_id=1, source_target_pairs={{0,2},{1,3},{2,0},{3,1},{4,6},{5,7},{6,4},{7,5},{8,10},{9,11},{10,... | collective-permute-start | bytes 196616 | tf_op jit(solution)/shard_map/ppermute | solution.py:168
  61.1 5.6 %collective-permute-start.11 = (f16[64,512]{1,0:T(8,128)(2,1)S(1)}, f16[64,512]{1,0:T(8,128)(2,1)S(1)}, u32[]{:S(2)}, u32[]{:S(2)}) collective-permute-start(f16[64,512]{1,0:T(8,128)(2,1)S(1)} %fusion.16), channel_id=1, source_target_pairs={{0,2},{1,3},{2,0},{3,1},{4,6},{5,7},{6,4},{7,5},{8,10},{9,11},{10,... | collective-permute-start | bytes 196616 | tf_op jit(solution)/shard_map/ppermute | solution.py:168
  65.3 7.0 %collective-permute-start.16 = (f16[64,512]{1,0:T(8,128)(2,1)S(1)}, f16[64,512]{1,0:T(8,128)(2,1)S(1)}, u32[]{:S(2)}, u32[]{:S(2)}) collective-permute-start(f16[64,512]{1,0:T(8,128)(2,1)S(1)} %fusion.9), channel_id=1, source_target_pairs={{0,4},{1,5},{2,6},{3,7},{4,0},{5,1},{6,2},{7,3},{8,12},{9,13},{10,... | collective-permute-start | bytes 196616 | tf_op jit(solution)/shard_map/ppermute | solution.py:168
  66.7 6.3 %collective-permute-start.12 = (f16[64,512]{1,0:T(8,128)(2,1)S(1)}, f16[64,512]{1,0:T(8,128)(2,1)S(1)}, u32[]{:S(2)}, u32[]{:S(2)}) collective-permute-start(f16[64,512]{1,0:T(8,128)(2,1)S(1)} %fusion.8), channel_id=1, source_target_pairs={{0,4},{1,5},{2,6},{3,7},{4,0},{5,1},{6,2},{7,3},{8,12},{9,13},{10,... | collective-permute-start | bytes 196616 | tf_op jit(solution)/shard_map/ppermute | solution.py:168
  76.7 10.1 %collective-permute-start.19 = (f16[64,2048]{1,0:T(8,128)(2,1)S(1)}, f16[64,2048]{1,0:T(8,128)(2,1)S(1)}, u32[]{:S(2)}, u32[]{:S(2)}) collective-permute-start(f16[64,2048]{1,0:T(8,128)(2,1)S(1)} %convert_element_type.279), channel_id=1, source_target_pairs={{0,8},{8,16},{16,24},{24,0},{1,9},{9,17},{17,25},{25,1},{2,10},{10... | collective-permute-start | bytes 786440 | tf_op jit(solution)/shard_map/ppermute | solution.py:163
  77.9 13.7 %collective-permute-start.18 = (f16[64,2048]{1,0:T(8,128)(2,1)S(1)}, f16[64,2048]{1,0:T(8,128)(2,1)S(1)}, u32[]{:S(2)}, u32[]{:S(2)}) collective-permute-start(f16[64,2048]{1,0:T(8,128)(2,1)S(1)} %convert_element_type.276), channel_id=1, source_target_pairs={{0,8},{8,16},{16,24},{24,0},{1,9},{9,17},{17,25},{25,1},{2,10},{10... | collective-permute-start | bytes 786440 | tf_op jit(solution)/shard_map/ppermute | solution.py:163
  93.4 3.4 %collective-permute-start.20 = (f16[64,512]{1,0:T(8,128)(2,1)S(1)}, f16[64,512]{1,0:T(8,128)(2,1)S(1)}, u32[]{:S(2)}, u32[]{:S(2)}) collective-permute-start(f16[64,512]{1,0:T(8,128)(2,1)S(1)} %multiply_convert_fusion.9), channel_id=1, source_target_pairs={{0,1},{1,0},{2,3},{3,2},{4,5},{5,4},{6,7},{7,6},{8,9},{9,8},{10,11... | collective-permute-start | bytes 196616 | tf_op jit(solution)/shard_map/ppermute | solution.py:168
  95.5 5.0 %collective-permute-start.25 = (f16[64,512]{1,0:T(8,128)(2,1)S(1)}, f16[64,512]{1,0:T(8,128)(2,1)S(1)}, u32[]{:S(2)}, u32[]{:S(2)}) collective-permute-start(f16[64,512]{1,0:T(8,128)(2,1)S(1)} %fusion.19), channel_id=1, source_target_pairs={{0,2},{1,3},{2,0},{3,1},{4,6},{5,7},{6,4},{7,5},{8,10},{9,11},{10,... | collective-permute-start | bytes 196616 | tf_op jit(solution)/shard_map/ppermute | solution.py:168
  96.8 4.7 %collective-permute-start.21 = (f16[64,512]{1,0:T(8,128)(2,1)S(1)}, f16[64,512]{1,0:T(8,128)(2,1)S(1)}, u32[]{:S(2)}, u32[]{:S(2)}) collective-permute-start(f16[64,512]{1,0:T(8,128)(2,1)S(1)} %fusion.18), channel_id=1, source_target_pairs={{0,2},{1,3},{2,0},{3,1},{4,6},{5,7},{6,4},{7,5},{8,10},{9,11},{10,... | collective-permute-start | bytes 196616 | tf_op jit(solution)/shard_map/ppermute | solution.py:168
  100.5 6.7 %collective-permute-start.26 = (f16[64,512]{1,0:T(8,128)(2,1)S(1)}, f16[64,512]{1,0:T(8,128)(2,1)S(1)}, u32[]{:S(2)}, u32[]{:S(2)}) collective-permute-start(f16[64,512]{1,0:T(8,128)(2,1)S(1)} %fusion.11), channel_id=1, source_target_pairs={{0,4},{1,5},{2,6},{3,7},{4,0},{5,1},{6,2},{7,3},{8,12},{9,13},{10,... | collective-permute-start | bytes 196616 | tf_op jit(solution)/shard_map/ppermute | solution.py:168
  101.6 6.3 %collective-permute-start.22 = (f16[64,512]{1,0:T(8,128)(2,1)S(1)}, f16[64,512]{1,0:T(8,128)(2,1)S(1)}, u32[]{:S(2)}, u32[]{:S(2)}) collective-permute-start(f16[64,512]{1,0:T(8,128)(2,1)S(1)} %fusion.10), channel_id=1, source_target_pairs={{0,4},{1,5},{2,6},{3,7},{4,0},{5,1},{6,2},{7,3},{8,12},{9,13},{10,... | collective-permute-start | bytes 196616 | tf_op jit(solution)/shard_map/ppermute | solution.py:168
  111.6 10.1 %collective-permute-start.29 = (f16[64,2048]{1,0:T(8,128)(2,1)S(1)}, f16[64,2048]{1,0:T(8,128)(2,1)S(1)}, u32[]{:S(2)}, u32[]{:S(2)}) collective-permute-start(f16[64,2048]{1,0:T(8,128)(2,1)S(1)} %convert_element_type.299), channel_id=1, source_target_pairs={{0,8},{8,16},{16,24},{24,0},{1,9},{9,17},{17,25},{25,1},{2,10},{10... | collective-permute-start | bytes 786440 | tf_op jit(solution)/shard_map/ppermute | solution.py:163
  112.2 14.3 %collective-permute-start.28 = (f16[64,2048]{1,0:T(8,128)(2,1)S(1)}, f16[64,2048]{1,0:T(8,128)(2,1)S(1)}, u32[]{:S(2)}, u32[]{:S(2)}) collective-permute-start(f16[64,2048]{1,0:T(8,128)(2,1)S(1)} %convert_element_type.296), channel_id=1, source_target_pairs={{0,8},{8,16},{16,24},{24,0},{1,9},{9,17},{17,25},{25,1},{2,10},{10... | collective-permute-start | bytes 786440 | tf_op jit(solution)/shard_map/ppermute | solution.py:163
  130.4 5.0 %collective-permute-start.35 = (f16[64,512]{1,0:T(8,128)(2,1)S(1)}, f16[64,512]{1,0:T(8,128)(2,1)S(1)}, u32[]{:S(2)}, u32[]{:S(2)}) collective-permute-start(f16[64,512]{1,0:T(8,128)(2,1)S(1)} %fusion.21), channel_id=1, source_target_pairs={{0,2},{1,3},{2,0},{3,1},{4,6},{5,7},{6,4},{7,5},{8,10},{9,11},{10,... | collective-permute-start | bytes 196616 | tf_op jit(solution)/shard_map/ppermute | solution.py:168
  131.7 4.7 %collective-permute-start.31 = (f16[64,512]{1,0:T(8,128)(2,1)S(1)}, f16[64,512]{1,0:T(8,128)(2,1)S(1)}, u32[]{:S(2)}, u32[]{:S(2)}) collective-permute-start(f16[64,512]{1,0:T(8,128)(2,1)S(1)} %fusion.20), channel_id=1, source_target_pairs={{0,2},{1,3},{2,0},{3,1},{4,6},{5,7},{6,4},{7,5},{8,10},{9,11},{10,... | collective-permute-start | bytes 196616 | tf_op jit(solution)/shard_map/ppermute | solution.py:168
  135.4 6.7 %collective-permute-start.36 = (f16[64,512]{1,0:T(8,128)(2,1)S(1)}, f16[64,512]{1,0:T(8,128)(2,1)S(1)}, u32[]{:S(2)}, u32[]{:S(2)}) collective-permute-start(f16[64,512]{1,0:T(8,128)(2,1)S(1)} %fusion.13), channel_id=1, source_target_pairs={{0,4},{1,5},{2,6},{3,7},{4,0},{5,1},{6,2},{7,3},{8,12},{9,13},{10,... | collective-permute-start | bytes 196616 | tf_op jit(solution)/shard_map/ppermute | solution.py:168
  136.5 6.3 %collective-permute-start.32 = (f16[64,512]{1,0:T(8,128)(2,1)S(1)}, f16[64,512]{1,0:T(8,128)(2,1)S(1)}, u32[]{:S(2)}, u32[]{:S(2)}) collective-permute-start(f16[64,512]{1,0:T(8,128)(2,1)S(1)} %fusion.12), channel_id=1, source_target_pairs={{0,4},{1,5},{2,6},{3,7},{4,0},{5,1},{6,2},{7,3},{8,12},{9,13},{10,... | collective-permute-start | bytes 196616 | tf_op jit(solution)/shard_map/ppermute | solution.py:168
  146.5 8.4 %collective-permute-start.41 = (bf16[64,2048]{1,0:T(8,128)(2,1)S(1)}, bf16[64,2048]{1,0:T(8,128)(2,1)S(1)}, u32[]{:S(2)}, u32[]{:S(2)}) collective-permute-start(bf16[64,2048]{1,0:T(8,128)(2,1)S(1)} %convert_element_type.317), channel_id=1, source_target_pairs={{0,8},{8,0},{16,24},{24,16},{1,9},{9,1},{17,25},{25,17},{2,10},{10... | collective-permute-start | bytes 786440 | tf_op jit(solution)/shard_map/ppermute | solution.py:168
  147.1 10.0 %collective-permute-start.38 = (bf16[64,2048]{1,0:T(8,128)(2,1)S(1)}, bf16[64,2048]{1,0:T(8,128)(2,1)S(1)}, u32[]{:S(2)}, u32[]{:S(2)}) collective-permute-start(bf16[64,2048]{1,0:T(8,128)(2,1)S(1)} %convert_element_type.316), channel_id=1, source_target_pairs={{0,16},{8,24},{16,0},{24,8},{1,17},{9,25},{17,1},{25,9},{2,18},{10... | collective-permute-start | bytes 786440 | tf_op jit(solution)/shard_map/ppermute | solution.py:168
  148.7 13.2 %collective-permute-start.43 = (bf16[64,2048]{1,0:T(8,128)(2,1)S(1)}, bf16[64,2048]{1,0:T(8,128)(2,1)S(1)}, u32[]{:S(2)}, u32[]{:S(2)}) collective-permute-start(bf16[64,2048]{1,0:T(8,128)(2,1)S(1)} %convert_element_type.317), channel_id=1, source_target_pairs={{0,16},{8,24},{16,0},{24,8},{1,17},{9,25},{17,1},{25,9},{2,18},{10... | collective-permute-start | bytes 786440 | tf_op jit(solution)/shard_map/ppermute | solution.py:168
  154.9 11.9 %collective-permute-start.42 = (bf16[64,2048]{1,0:T(8,128)(2,1)S(1)}, bf16[64,2048]{1,0:T(8,128)(2,1)S(1)}, u32[]{:S(2)}, u32[]{:S(2)}) collective-permute-start(bf16[64,2048]{1,0:T(8,128)(2,1)S(1)} %collective-permute-done.41), channel_id=1, source_target_pairs={{0,16},{8,24},{16,0},{24,8},{1,17},{9,25},{17,1},{25,9},{2,18},{10... | collective-permute-start | bytes 786440 | tf_op jit(solution)/shard_map/ppermute | solution.py:168
  156.8 10.2 %collective-permute-start.40 = (bf16[64,2048]{1,0:T(8,128)(2,1)S(1)}, bf16[64,2048]{1,0:T(8,128)(2,1)S(1)}, u32[]{:S(2)}, u32[]{:S(2)}) collective-permute-start(bf16[64,2048]{1,0:T(8,128)(2,1)S(1)} %convert_element_type.316), channel_id=1, source_target_pairs={{0,8},{8,0},{16,24},{24,16},{1,9},{9,1},{17,25},{25,17},{2,10},{10... | collective-permute-start | bytes 786440 | tf_op jit(solution)/shard_map/ppermute | solution.py:168
  157.2 12.6 %collective-permute-start.39 = (bf16[64,2048]{1,0:T(8,128)(2,1)S(1)}, bf16[64,2048]{1,0:T(8,128)(2,1)S(1)}, u32[]{:S(2)}, u32[]{:S(2)}) collective-permute-start(bf16[64,2048]{1,0:T(8,128)(2,1)S(1)} %collective-permute-done.38), channel_id=1, source_target_pairs={{0,8},{8,0},{16,24},{24,16},{1,9},{9,1},{17,25},{25,17},{2,10},{10... | collective-permute-start | bytes 786440 | tf_op jit(solution)/shard_map/ppermute | solution.py:168
  (14 other events, 29.3 us)
